TPU v7x, 256 devices: a whole 4x4x8 slice. The times are simulated.
256 devices in a mesh: batch: 8 (over y, core), proto: 32 (over x, z).
Axes of the slice: x: 4, y: 4, z: 8, core: 2. Of those that a mesh axis runs over, the one named last changes fastest.
Arguments:
- student_feats: bfloat16 [16384, 256], P(('batch', 'proto')), may hold values from -0.375 to 0.375
- teacher_feats: bfloat16 [16384, 256], P(('batch', 'proto')), may hold values from -0.375 to 0.375
- student_protos: bfloat16 [256, 65536], P(None, 'proto'), may hold values from -1.5 to 1.5
- teacher_protos: bfloat16 [256, 65536], P(None, 'proto'), may hold values from -1.5 to 1.5
Outputs:
- proto_grad: float32 [256, 65536], P('batch', 'proto')
- feature_grad: float32 [16384, 256], P(('batch', 'proto'))
All inputs are finite; a program needn't handle non-finite values.
Results may differ from a plain program's by a relative error of at most 0.0089.
Values may be sent and summed in bfloat16 or wider, within the bound.
A program may use at most 128 MiB of HBM per device.

v0:
```python
import jax
import jax.numpy as jnp
from jax import lax
from jax.sharding import PartitionSpec as P

ITERS = 3


student_temp = 0.1
teacher_temp = 0.07


def unit_rows(feats):
    values = feats.astype(jnp.float32)
    norm = jnp.sqrt(jnp.sum(values * values, axis=1, keepdims=True) + 1e-06)
    return (values / norm, norm)


def shards(student_feats, teacher_feats, student_protos, teacher_protos):
    stud_all, teach_all = (
        lax.all_gather(student_feats, "proto", axis=0, tiled=True),
        lax.all_gather(teacher_feats, "proto", axis=0, tiled=True),
    )
    stud_unit, stud_norm = unit_rows(stud_all)
    stud_half = stud_unit.astype(jnp.bfloat16)
    teach_unit, teach_norm = unit_rows(teach_all)
    teach_half = teach_unit.astype(jnp.bfloat16)
    logits = jnp.dot(stud_half, student_protos, preferred_element_type=jnp.float32) / student_temp
    masses = jnp.exp(
        jnp.dot(teach_half, teacher_protos, preferred_element_type=jnp.float32) / teacher_temp
    )
    exp_local = jnp.sum(jnp.exp(logits), axis=1)
    crop_scale = jnp.ones((stud_all.shape[0],), jnp.float32)
    proto_scale = jnp.ones((masses.shape[1],), jnp.float32)
    exp_total = exp_local
    for step in range(ITERS):
        proto_sum = lax.psum(jnp.dot(crop_scale, masses, precision=lax.Precision.HIGHEST), "batch")
        proto_scale = 1.0 / proto_sum
        crop_local = jnp.dot(masses, proto_scale, precision=lax.Precision.HIGHEST)
        if step == 0:
            exp_total = lax.psum(exp_local, "proto")
            crop_sum = lax.psum(crop_local, "proto")
        else:
            crop_sum = lax.psum(crop_local, "proto")
        crop_scale = 1.0 / crop_sum
    lse = jnp.log(exp_total)
    probs = jnp.exp(logits - lse[:, None])
    targets = masses * crop_scale[:, None] * proto_scale[None, :]
    grad_half = (probs - targets).astype(jnp.bfloat16)
    proto_grad = lax.psum_scatter(
        lax.dot_general(
            stud_half, grad_half, (((0,), (0,)), ((), ())), preferred_element_type=jnp.float32
        )
        / student_temp,
        "batch",
        scatter_dimension=0,
        tiled=True,
    )
    owned = student_feats.shape[0]
    partial_grad = (
        lax.dot_general(
            grad_half, student_protos, (((1,), (1,)), ((), ())), preferred_element_type=jnp.float32
        )
        / student_temp
    )
    total_grad = lax.psum(partial_grad, "proto")
    inner = jnp.sum(stud_unit * total_grad, axis=1, keepdims=True)
    every_grad = (total_grad - stud_unit * inner) / stud_norm
    begin = lax.axis_index("proto") * owned
    feature_grad = lax.dynamic_slice_in_dim(every_grad, begin, owned, 0)
    return (proto_grad, feature_grad)


def solution(mesh):
    in_specs = (
        P(("batch", "proto"), None),
        P(("batch", "proto"), None),
        P(None, "proto"),
        P(None, "proto"),
    )
    out_specs = (P("batch", "proto"), P(("batch", "proto"), None))
    return jax.shard_map(shards, mesh=mesh, in_specs=in_specs, out_specs=out_specs, check_vma=False)
```

profile of v0, /device:TPU:1, one launch (start us, length us, event | category | flops | bytes accessed | tf_op | source)
XLA Modules:
  0.0 725.8 jit_solution(18087475396892012647)
XLA Ops:
  7.2 0.0 copy-start
  7.2 0.0 all-gather.5.cloned.1.call-start
  7.2 0.7 all-gather.5.cloned.1.call-update
  7.9 0.0 all-gather.3.cloned.1.call-start
  8.0 0.7 all-gather.3.cloned.1.call-update
  8.7 0.0 all-reduce.3.cloned.1.call-start
  8.7 77.5 %all-gather.5.cloned.1.call-done = bf16[2048,256]{1,0:T(8,128)(2,1)} async-done(((bf16[64,256]{1,0:T(8,128)(2,1)}), bf16[2048,256]{1,0:T(8,128)(2,1)}) %all-gather.5.cloned.1.call-update) | async-done | bytes 1048592 | tf_op jit(solution)/shard_map/all_gather | solution.py:22
  86.2 1.6 fusion.1
  87.8 4.6 multiply_exponential_fusion
  92.4 0.0 copy-start.1
  92.4 5.7 copy-done.1
  98.1 13.9 %fusion.9 = f32[1,2048]{1,0:T(1,128)S(1)} fusion(f32[2048,2048]{0,1:T(8,128)S(1)} %multiply_exponential_fusion), kind=kOutput, calls=%fused_computation.22 | convolution fusion | flops 50331648 | bytes 16785408 | tf_op jit(solution)/shard_map/dot_general | solution.py:37
  112.0 17.0 %psum.57 = f32[2048]{0:T(1024)S(1)} all-reduce(f32[2048]{0:T(1024)S(1)} %bitcast.37), channel_id=1, replica_groups=mesh['batch'=8,'proto'=32] {'batch'}, use_global_device_ids=true, to_apply=%region_4.0 | all-reduce | flops 2048 | bytes 16384 | tf_op jit(solution)/shard_map/psum | solution.py:37
  129.0 12.5 %fusion.12 = f32[1,2048]{1,0:T(1,128)S(1)} fusion(f32[2048,2048]{0,1:T(8,128)} %copy-done.1, f32[2048,1]{0,1:T(1,128)S(1)} %bitcast.35), kind=kOutput, calls=%fused_computation.31 | convolution fusion | flops 50331648 | bytes 16793600 | tf_op jit(solution)/shard_map/dot_general | solution.py:39
  141.5 59.5 %psum.58 = f32[2048]{0:T(1024)S(1)} all-reduce(f32[2048]{0:T(1024)S(1)} %bitcast.29), channel_id=1, replica_groups=mesh['batch'=8,'proto'=32] {'proto'}, use_global_device_ids=true, to_apply=%region_5.0 | all-reduce | flops 2048 | bytes 16384 | tf_op jit(solution)/shard_map/psum | solution.py:42
  201.0 17.0 %fusion.13 = f32[1,2048]{1,0:T(1,128)S(1)} fusion(f32[2048,1]{0,1:T(1,128)S(1)} %bitcast.31, f32[2048,2048]{0,1:T(8,128)} %copy-done.1), kind=kOutput, calls=%fused_computation.32 | convolution fusion | flops 50331648 | bytes 16793600 | tf_op jit(solution)/shard_map/dot_general | solution.py:37
  218.0 26.9 %psum.59 = f32[2048]{0:T(1024)S(1)} all-reduce(f32[2048]{0:T(1024)S(1)} %bitcast.32), channel_id=1, replica_groups=mesh['batch'=8,'proto'=32] {'batch'}, use_global_device_ids=true, to_apply=%region_6.0 | all-reduce | flops 2048 | bytes 16384 | tf_op jit(solution)/shard_map/psum | solution.py:37
  244.9 12.6 %fusion.14 = f32[1,2048]{1,0:T(1,128)S(1)} fusion(f32[2048,2048]{0,1:T(8,128)} %copy-done.1, f32[2048,1]{0,1:T(1,128)S(1)} %bitcast.36), kind=kOutput, calls=%fused_computation.33 | convolution fusion | flops 50331648 | bytes 16793600 | tf_op jit(solution)/shard_map/dot_general | solution.py:39
  257.6 56.7 %psum.60 = f32[2048]{0:T(1024)S(1)} all-reduce(f32[2048]{0:T(1024)S(1)} %bitcast.30), channel_id=1, replica_groups=mesh['batch'=8,'proto'=32] {'proto'}, use_global_device_ids=true, to_apply=%region_7.0 | all-reduce | flops 2048 | bytes 16384 | tf_op jit(solution)/shard_map/psum | solution.py:44
  314.4 17.0 %fusion.15 = f32[1,2048]{1,0:T(1,128)S(1)} fusion(f32[2048,1]{0,1:T(1,128)S(1)} %bitcast.33, f32[2048,2048]{0,1:T(8,128)} %copy-done.1), kind=kOutput, calls=%fused_computation.34 | convolution fusion | flops 50331648 | bytes 16793600 | tf_op jit(solution)/shard_map/dot_general | solution.py:37
  331.4 26.6 %psum.61 = f32[2048]{0:T(1024)S(1)} all-reduce(f32[2048]{0:T(1024)S(1)} %bitcast.34), channel_id=1, replica_groups=mesh['batch'=8,'proto'=32] {'batch'}, use_global_device_ids=true, to_apply=%region_8.0 | all-reduce | flops 2048 | bytes 16384 | tf_op jit(solution)/shard_map/psum | solution.py:37
  358.0 12.4 %fusion.16 = f32[1,2048]{1,0:T(1,128)S(1)} fusion(f32[2048,2048]{0,1:T(8,128)} %copy-done.1, f32[2048,1]{0,1:T(1,128)S(1)} %bitcast.27), kind=kOutput, calls=%fused_computation.35 | convolution fusion | flops 50331648 | bytes 16793600 | tf_op jit(solution)/shard_map/dot_general | solution.py:39
  370.4 0.0 all-gather.3.cloned.1.call-done
  370.4 1.6 fusion
  372.0 0.0 copy-done
  372.0 8.6 %exponential_reduce_fusion = (f32[2048]{0:T(1024)S(1)}, f32[2048,2048]{0,1:T(8,128)}) fusion(bf16[256,2048]{1,0:T(8,128)(2,1)S(1)} %copy-done, f32[2048]{0:T(1024)S(1)} %add_sqrt_fusion.1, bf16[2048,256]{1,0:T(8,128)(2,1)} %all-gather.3.cloned.1.call-done), kind=kOutput, calls=%fused_computation.2 | convolution fusion | flops 2157443072 | bytes 18890752 | tf_op jit(solution)/shard_map/dot_general | solution.py:28
  380.7 111.8 %all-reduce = (f32[2048]{0:T(1024)S(1)}, f32[2048]{0:T(1024)S(1)}) all-reduce(f32[2048]{0:T(1024)S(1)} %bitcast.28, f32[2048]{0:T(1024)S(1)} %get-tuple-element.6), channel_id=1, replica_groups=mesh['batch'=8,'proto'=32] {'proto'}, use_global_device_ids=true, to_apply=%region_9.0 | all-reduce | flops 4096 | bytes 32768 | tf_op jit(solution)/shard_map/psum | solution.py:44
  492.5 12.4 %subtract_convert_fusion = bf16[2048,2048]{0,1:T(8,128)(2,1)S(1)} fusion(f32[2048,2048]{0,1:T(8,128)} %copy-done.1, f32[2048,2048]{0,1:T(8,128)} %get-tuple-element.7, f32[2048]{0:T(1024)S(1)} %broadcast_divide_fusion, f32[2048]{0:T(1024)S(1)} %broadcast_divide_fusion.5, f32[2048]{0:T(1024)S(1)} %log.3), kind=kLoop, calls=%fused_computation | loop fusion | flops 25165824 | bytes 41967616 | tf_op jit(solution)/shard_map/convert_element_type | solution.py:49
  504.9 0.0 copy-start.2
  504.9 3.2 copy-done.2
  508.1 0.0 copy-start.3
  508.1 4.0 convolution_multiply_fusion
  512.1 0.0 all-reduce.3.cloned.1.call-update
  512.1 0.3 reduce-scatter.2.cloned.1.call-start
  512.4 0.0 copy-done.3
  512.4 7.5 %convolution_multiply_fusion.1 = f32[256,2048]{1,0:T(8,128)} fusion(bf16[2048,2048]{0,1:T(8,128)(2,1)} %copy-done.2, bf16[2048,256]{1,0:T(8,128)(2,1)S(1)} %copy-done.3, f32[2048]{0:T(1024)S(1)} %add_sqrt_fusion.1), kind=kOutput, calls=%fused_computation.4 | convolution fusion | flops 2149580800 | bytes 11542528 | tf_op jit(solution)/shard_map/dot_general | solution.py:51
  519.9 0.0 reduce-scatter.2.cloned.1.call-update
  519.9 0.1 dynamic-slice.1
  520.0 160.7 %all-reduce.3.cloned.1.call-done = f32[2048,256]{1,0:T(8,128)} async-done(((f32[2048,256]{1,0:T(8,128)}), f32[2048,256]{1,0:T(8,128)}) %all-reduce.3.cloned.1.call-update) | async-done | bytes 2097168 | tf_op jit(solution)/shard_map/psum | solution.py:66
  680.7 2.2 multiply_reduce_fusion
  683.0 0.1 dynamic-slice
  683.0 1.6 fusion.8
  684.6 34.4 %reduce-scatter.2.cloned.1.call-done = f32[32,2048]{1,0:T(8,128)} async-done(((f32[256,2048]{1,0:T(8,128)}), f32[32,2048]{1,0:T(8,128)}) %reduce-scatter.2.cloned.1.call-update) | async-done | bytes 262160 | tf_op jit(solution)/shard_map/reduce_scatter | solution.py:50
  (9 shorter events, 0.0 us)
Async XLA Ops:
  7.2 364.9 %copy-start = (bf16[256,2048]{1,0:T(8,128)(2,1)S(1)}, bf16[256,2048]{1,0:T(8,128)(2,1)}, u32[]{:S(2)}) copy-start(bf16[256,2048]{1,0:T(8,128)(2,1)} %param.6) | copy-start | bytes 3145732
  7.2 79.0 %all-gather.5.cloned.1.call-start = ((), (), s32[]{:S(2)}) async-start(), calls=%async_computation.2 | async-start | bytes 1081344 | tf_op jit(solution)/shard_map/all_gather | solution.py:22
  7.9 362.5 %all-gather.3.cloned.1.call-start = ((), (), s32[]{:S(2)}) async-start(), calls=%async_computation.1 | async-start | bytes 1081344 | tf_op jit(solution)/shard_map/all_gather | solution.py:21
  8.7 672.1 %all-reduce.3.cloned.1.call-start = ((), (), s32[]{:S(2)}) async-start(), calls=%async_computation.4 | async-start | bytes 4194304 | tf_op jit(solution)/shard_map/psum | solution.py:66
  92.4 5.7 copy-start.1
  504.9 3.2 copy-start.2
  508.1 4.3 copy-start.3
  512.1 206.9 %reduce-scatter.2.cloned.1.call-start = ((), (), s32[]{:S(2)}) async-start(), calls=%async_computation.3 | async-start | bytes 2359296 | tf_op jit(solution)/shard_map/reduce_scatter | solution.py:50
Sparse Core Ops, SparseCore 0:
  10.6 75.5 all-gather.4
  88.8 73.9 all-gather.2
  512.2 168.4 all-reduce.2
  683.9 35.0 reduce-scatter.1
where the time goes:
time: 737 us; the launch traced here: 726 us
  blocking collectives  299 us (41%)
  waiting for transfers between devices  274 us (37%)
  matrix products  110 us (15%)
  other arithmetic  19.4 us (3%)
  between operations  14.2 us (2%)
  local copies, waits for them, and re-layouts  9.1 us (1%)
    psum x3, blocking collectives, shards(): crop_sum = lax.psum(crop_local, 'proto')  228 us
    psum x1, waiting for transfers between devices, shards(): total_grad = lax.psum(partial_grad, 'proto')  161 us
    all_gather x1, waiting for transfers between devices, shards(): lax.all_gather(teacher_feats, 'proto', axis=0, tiled=True)  77.5 us
    psum x3, blocking collectives, shards(): lax.psum(jnp.dot(crop_scale, masses, precision=lax.Precision.HIGHEST), 'b...  70.5 us
    dot_general x3, matrix products, shards(): jnp.dot(crop_scale, masses, precision=lax.Precision.HIGHEST)  48 us
    dot_general x3, matrix products, shards(): crop_local = jnp.dot(masses, proto_scale, precision=lax.Precision.HIGHEST)  37.5 us
    reduce_scatter x1, waiting for transfers between devices, shards(): lax.psum_scatter(lax.dot_general(stud_half, grad_half, (((0,), (0,)), (()...  34.4 us
  transfers between devices with their start and end apart: 4, of which 3 were waited for; matrix products, arithmetic and copies ran while one was open for 14% of the time, Pallas kernels for 0%

commit v1 on v0

v1 whole, which is shorter than its diff:
```python
import functools

import jax
import jax.numpy as jnp
from jax import lax
from jax.experimental import pallas as pl
from jax.experimental.pallas import tpu as pltpu
from jax.sharding import PartitionSpec as P

ITERS = 3
STUDENT_TEMP = 0.1
TEACHER_TEMP = 0.07
LOG2E = 1.4426950408889634
MESH = pl.DeviceIdType.MESH
F32 = jnp.float32
BF16 = jnp.bfloat16
LANES = 128


def unit_rows(feats):
    values = feats.astype(F32)
    norm = jnp.sqrt(jnp.sum(values * values, axis=1, keepdims=True) + 1e-06)
    return values / norm, norm


def kernel(
    nx, nz, ny,
    sf, tf, sp_hbm, tp_hbm,
    pg_out, fg_out,
    tp, sp, spt, tall, uall, ut, m, e, g,
    colacc, ps, payload, cinv, ccs,
    cb, xb, zb_sum, zb,
    ugb, xr, zs, zr,
    pgf, pgb, cr, ys, yr,
    local_s,
    tx_s, tx_r, tr_s, tr_r, tl_s, tl_r,
    ur_s, ur_r, ul_s, ul_r, ux_s, ux_r,
    cb_s, cb_r, ax_s, ax_r, az_s, az_r,
    fx_s, fx_r, fz_s, fz_r, pc_s, pc_r, py_s, py_r,
):
    rows = sf.shape[0]
    depth, width = tp.shape
    block = nx * rows
    crops = nz * block
    nb = 2 * ny
    dr = depth // nb
    tile = min(256, width)
    groups = crops // LANES
    per = block // LANES
    chunk = min(512, width)

    pid = lax.axis_index("proto")
    bid = lax.axis_index("batch")
    x, z = pid // nz, pid % nz
    y, c = bid // 2, bid % 2
    my = pl.multiple_of(x * rows, rows)

    def to_xz(xx, zz):
        return {"proto": (xx % nx) * nz + zz % nz}

    def to_b(bb):
        return {"batch": bb % nb}

    def remote(src, dst, ss, rs, dev):
        return pltpu.make_async_remote_copy(
            src_ref=src, dst_ref=dst, send_sem=ss, recv_sem=rs, device_id=dev, device_id_type=MESH
        )

    barrier = pltpu.get_barrier_semaphore()
    for k in range(1, nx):
        pl.semaphore_signal(barrier, inc=1, device_id=to_xz(x + k, z), device_id_type=MESH)
    for k in range(1, nz):
        pl.semaphore_signal(barrier, inc=1, device_id=to_xz(x, z + k), device_id_type=MESH)
    for k in range(1, nb):
        pl.semaphore_signal(barrier, inc=1, device_id=to_b(bid + k), device_id_type=MESH)

    load_tp = pltpu.make_async_copy(tp_hbm, tp, local_s.at[0])
    load_sp = pltpu.make_async_copy(sp_hbm, sp, local_s.at[1])
    load_tp.start()
    load_sp.start()

    tall[z, pl.ds(my, rows), :] = unit_rows(tf[...])[0].astype(BF16)
    uall[z, pl.ds(my, rows), :] = unit_rows(sf[...])[0].astype(BF16)
    colacc[...] = jnp.zeros_like(colacc)
    eye = lax.broadcasted_iota(jnp.int32, (LANES, LANES), 0) == lax.broadcasted_iota(
        jnp.int32, (LANES, LANES), 1
    )

    def to_row(col):
        return jnp.sum(jnp.where(eye, col, 0.0), axis=0, keepdims=True)

    def to_col(row):
        return jnp.sum(jnp.where(eye, row, 0.0), axis=1, keepdims=True)

    pl.semaphore_wait(barrier, (nx - 1) + (nz - 1) + (nb - 1))

    half = nz // 2

    def tx(k):
        ref = tall.at[z, pl.ds(my, rows)]
        return remote(ref, ref, tx_s.at[k - 1], tx_r.at[k - 1], to_xz(x + k, z))

    def tright(s):
        ref = tall.at[(z - s + nz) % nz]
        return remote(ref, ref, tr_s.at[s], tr_r.at[s], to_xz(x, z + 1))

    def tleft(s):
        ref = tall.at[(z + s) % nz]
        return remote(ref, ref, tl_s.at[s], tl_r.at[s], to_xz(x, z + nz - 1))

    def uright(s):
        ref = uall.at[(z - s + nz) % nz, pl.ds(my, rows)]
        return remote(ref, ref, ur_s.at[s], ur_r.at[s], to_xz(x, z + 1))

    def uleft(s):
        ref = uall.at[(z + s) % nz, pl.ds(my, rows)]
        return remote(ref, ref, ul_s.at[s], ul_r.at[s], to_xz(x, z + nz - 1))

    def ux(off, k):
        ref = uall.at[(z + off) % nz, pl.ds(my, rows)]
        return remote(
            ref, ref, ux_s.at[off * (nx - 1) + k - 1], ux_r.at[off * (nx - 1) + k - 1], to_xz(x + k, z)
        )

    for k in range(1, nx):
        tx(k).start()
    uright(0).start()
    if half > 1:
        uleft(0).start()
    for k in range(1, nx):
        ux(0, k).start()

    def compute_m(blk):
        row0 = pl.multiple_of(blk * block, block)
        a = tall[blk]
        for j in range(width // tile):
            cols = slice(j * tile, (j + 1) * tile)
            s = jnp.dot(a, tp[:, cols], preferred_element_type=F32)
            v = jnp.exp2(s * (LOG2E / TEACHER_TEMP))
            m[pl.ds(row0, block), cols] = v
            colacc[:, cols] += jnp.sum(v.reshape(block // 8, 8, tile), axis=0)

    for k in range(1, nx):
        tx(k).wait_recv()
    tright(0).start()
    if half > 1:
        tleft(0).start()
    load_tp.wait()
    compute_m(z)

    @pl.loop(0, half)
    def _(s):
        tright(s).wait_recv()

        @pl.when(s < half - 1)
        def _():
            tright(s + 1).start()
            tleft(s).wait_recv()

        @pl.when(s < half - 2)
        def _():
            tleft(s + 1).start()

        uright(s).wait_recv()

        @pl.when(s < half - 1)
        def _():
            uright(s + 1).start()
            uleft(s).wait_recv()

        @pl.when(s < half - 2)
        def _():
            uleft(s + 1).start()

        for k in range(1, nx):
            ux(nz - 1 - s, k).start()

        @pl.when(s < half - 1)
        def _():
            for k in range(1, nx):
                ux(s + 1, k).start()

        @pl.loop(0, jnp.where(s < half - 1, 2, 1))
        def _(k):
            off = jnp.where(k == 0, nz - 1 - s, 1 + s)
            compute_m((z + off) % nz)

    def cb_copy(it, k):
        return remote(
            ps.at[it], cb.at[it, k - 1], cb_s.at[it, k - 1], cb_r.at[it, k - 1], to_b(bid + k)
        )

    def ax_copy(it, k):
        n = groups if it < ITERS - 1 else 2 * groups
        return remote(
            payload.at[it, pl.ds(0, n)], xb.at[it, k - 1, pl.ds(0, n)],
            ax_s.at[it, k - 1], ax_r.at[it, k - 1], to_xz(x + k, z),
        )

    def az_copy(it, k):
        n = groups if it < ITERS - 1 else 2 * groups
        return remote(
            zb_sum.at[it, pl.ds(0, n)], zb.at[it, k - 1, pl.ds(0, n)],
            az_s.at[it, k - 1], az_r.at[it, k - 1], to_xz(x, z + k),
        )

    def compute_e(blk):
        row0 = pl.multiple_of(blk * block, block)
        a = uall[blk]
        acc = jnp.zeros((block, LANES), F32)
        for j in range(width // tile):
            cols = slice(j * tile, (j + 1) * tile)
            s = jnp.dot(a, sp[:, cols], preferred_element_type=F32)
            v = jnp.exp2(jnp.minimum(s * (LOG2E / STUDENT_TEMP) - 2.0, 127.0))
            e[pl.ds(row0, block), cols] = v
            for t in range(tile // LANES):
                acc += v[:, t * LANES : (t + 1) * LANES]
        for i in range(per):
            col = jnp.sum(acc[i * LANES : (i + 1) * LANES], axis=1, keepdims=True)
            payload[ITERS - 1, pl.ds(groups + blk * per + i, 1), :] = to_row(col)

    def e_blocks(lo, hi):
        @pl.loop(lo, hi)
        def _(k):
            compute_e((z + k) % nz)

    def colsum():
        def body(i, acc):
            col = to_col(ccs[pl.ds(i, 1), :])
            for q in range(LANES // 8):
                acc = acc + m[pl.ds(i * LANES + q * 8, 8), :] * col[q * 8 : (q + 1) * 8]
            return acc

        return lax.fori_loop(0, groups, body, jnp.zeros((8, width), F32))

    def rowsum(it, scale):
        @pl.loop(0, groups)
        def _(i):
            acc = jnp.zeros((LANES, LANES), F32)
            for t in range(width // LANES):
                cols = slice(t * LANES, (t + 1) * LANES)
                acc = acc + m[pl.ds(i * LANES, LANES), cols] * scale[:, cols]
            col = jnp.sum(acc, axis=1, keepdims=True)
            payload[it, pl.ds(i, 1), :] = to_row(col)

    cuts = [nz * i // 8 for i in range(9)]
    for it in range(ITERS):
        part = colacc[...] if it == 0 else colsum()
        ps[it] = jnp.sum(part, axis=0, keepdims=True)
        for k in range(1, nb):
            cb_copy(it, k).start()
        if it == 0:
            load_sp.wait()
            for off in range(nz):
                for k in range(1, nx):
                    ux(off, k).wait_recv()
            e_blocks(cuts[0], cuts[2])
        elif it == 1:
            e_blocks(cuts[5], cuts[7])
        else:

            @pl.loop(0, nz)
            def _(k):
                ut[:, pl.ds(pl.multiple_of(k * block, block), block)] = uall[k].T

        for k in range(1, nb):
            cb_copy(it, k).wait_recv()
        total = ps[it]
        for k in range(1, nb):
            total = total + cb[it, k - 1]
        scale = 1.0 / total
        rowsum(it, scale)
        if it == ITERS - 1:
            cps = scale
        for k in range(1, nx):
            ax_copy(it, k).start()
        if it == 0:
            e_blocks(cuts[2], cuts[3])
        elif it == 1:
            e_blocks(cuts[7], cuts[8])
        for k in range(1, nx):
            ax_copy(it, k).wait_recv()
        n = groups if it < ITERS - 1 else 2 * groups
        total = payload[it, pl.ds(0, n)]
        for k in range(1, nx):
            total = total + xb[it, k - 1, pl.ds(0, n)]
        zb_sum[it, pl.ds(0, n)] = total
        for k in range(1, nz):
            az_copy(it, k).start()
        if it == 0:
            e_blocks(cuts[3], cuts[5])
        elif it == 1:

            @pl.loop(0, width // tile)
            def _(j):
                cols = pl.ds(pl.multiple_of(j * tile, tile), tile)
                spt[cols, :] = sp[:, cols].T

        for k in range(1, nz):
            az_copy(it, k).wait_recv()
        total = zb_sum[it, pl.ds(0, n)]
        for k in range(1, nz):
            total = total + zb[it, k - 1, pl.ds(0, n)]
        inverse = 1.0 / total
        ccs[...] = inverse[:groups]
        if it == ITERS - 1:
            cinv[...] = inverse[groups:]

    def order(s):
        return half + jnp.where(s % 2 == 0, s // 2, -((s + 1) // 2))

    def fx_copy(off, k):
        blk = (z + off) % nz
        xx = (x + k) % nx
        return remote(
            ugb.at[blk, pl.ds(pl.multiple_of(xx * rows, rows), rows)],
            xr.at[k - 1, blk],
            fx_s.at[off * (nx - 1) + k - 1], fx_r.at[off * (nx - 1) + k - 1], to_xz(xx, z),
        )

    def fz_copy(off):
        return remote(
            zs.at[off], zr.at[off - 1], fz_s.at[off - 1], fz_r.at[off - 1], to_xz(x, z + off)
        )

    @pl.loop(0, nz)
    def _(s):
        off = order(s)
        blk = (z + off) % nz
        row0 = pl.multiple_of(blk * block, block)
        inv = jnp.concatenate([to_col(cinv[pl.ds(blk * per + i, 1), :]) for i in range(per)], axis=0)
        sca = jnp.concatenate([to_col(ccs[pl.ds(blk * per + i, 1), :]) for i in range(per)], axis=0)
        acc = jnp.zeros((block, depth), F32)
        for j in range(width // tile):
            cols = slice(j * tile, (j + 1) * tile)
            prob = e[pl.ds(row0, block), cols] * inv
            target = (m[pl.ds(row0, block), cols] * sca) * cps[:, cols]
            gh = (prob - target).astype(BF16)
            g[pl.ds(row0, block), cols] = gh
            acc += jnp.dot(gh, spt[cols, :], preferred_element_type=F32)
        ugb[blk] = acc.astype(BF16)
        for k in range(1, nx):
            fx_copy(off, k).start()

    def pc_copy(j):
        cols = pl.ds(pl.multiple_of(j * chunk, chunk), chunk)
        return remote(
            pgb.at[1 - c, :, :, cols], cr.at[:, :, cols], pc_s.at[j], pc_r.at[j], to_b(y * 2 + 1 - c)
        )

    def py_copy(j, k):
        cols = pl.ds(pl.multiple_of(j * chunk, chunk), chunk)
        return remote(
            ys.at[k - 1, :, cols], yr.at[k - 1, :, cols],
            py_s.at[j, k - 1], py_r.at[j, k - 1], to_b(bid + 2 * k),
        )

    @pl.loop(0, width // chunk)
    def _(j):
        cols = pl.ds(pl.multiple_of(j * chunk, chunk), chunk)
        part = jnp.dot(ut[...], g[:, cols], preferred_element_type=F32)
        for yy in range(ny):
            for cc in range(2):
                d0 = (yy * 2 + cc) * dr
                pgf[cc, yy, :, cols] = part[d0 : d0 + dr]
                pgb[cc, yy, :, cols] = part[d0 : d0 + dr].astype(BF16)
        pc_copy(j).start()

    @pl.loop(0, nz)
    def _(s):
        off = order(s)
        blk = (z + off) % nz
        for k in range(1, nx):
            fx_copy(off, k).wait_recv()
        total = ugb[blk, pl.ds(my, rows), :].astype(F32)
        for k in range(1, nx):
            total = total + xr[k - 1, blk].astype(F32)
        zs[off] = total.astype(BF16)

        @pl.when(s < nz - 1)
        def _():
            fz_copy(off).start()

        nch = width // chunk

        @pl.when((s % 2 == 1) & (s // 2 < nch))
        def _():
            j = s // 2
            cols = pl.ds(pl.multiple_of(j * chunk, chunk), chunk)
            pc_copy(j).wait_recv()
            pg_out[:, cols] = pgf[c, y, :, cols] + cr[y, :, cols].astype(F32)
            for k in range(1, ny):
                yy = (y + k) % ny
                ys[k - 1, :, cols] = (pgf[c, yy, :, cols] + cr[yy, :, cols].astype(F32)).astype(BF16)
                py_copy(j, k).start()

    for off in range(1, nz):
        fz_copy(off).wait_recv()
    total = zs[0].astype(F32)
    for off in range(1, nz):
        total = total + zr[off - 1].astype(F32)
    total = total / STUDENT_TEMP
    unit, norm = unit_rows(sf[...])
    inner = jnp.sum(unit * total, axis=1, keepdims=True)
    fg_out[...] = (total - unit * inner) / norm

    @pl.loop(0, width // chunk)
    def _(j):
        cols = pl.ds(pl.multiple_of(j * chunk, chunk), chunk)
        total = pg_out[:, cols]
        for k in range(1, ny):
            py_copy(j, k).wait_recv()
            total = total + yr[k - 1, :, cols].astype(F32)
        pg_out[:, cols] = total / STUDENT_TEMP

    for k in range(1, nx):
        tx(k).wait_send()

    @pl.loop(0, half)
    def _(s):
        tright(s).wait_send()
        uright(s).wait_send()

        @pl.when(s < half - 1)
        def _():
            tleft(s).wait_send()
            uleft(s).wait_send()

    @pl.loop(0, nz)
    def _(off):
        for k in range(1, nx):
            ux(off, k).wait_send()
            fx_copy(off, k).wait_send()

        @pl.when(off > 0)
        def _():
            fz_copy(off).wait_send()

    for it in range(ITERS):
        for k in range(1, nb):
            cb_copy(it, k).wait_send()
        for k in range(1, nx):
            ax_copy(it, k).wait_send()
        for k in range(1, nz):
            az_copy(it, k).wait_send()

    @pl.loop(0, width // chunk)
    def _(j):
        pc_copy(j).wait_send()
        for k in range(1, ny):
            py_copy(j, k).wait_send()


def shards(nx, nz, ny, student_feats, teacher_feats, student_protos, teacher_protos):
    rows, depth = student_feats.shape
    width = student_protos.shape[1]
    block, nb = nx * rows, 2 * ny
    crops, dr = nz * block, depth // nb
    groups = crops // LANES
    chunk = min(512, width)
    nch = width // chunk
    half = nz // 2
    one = lambda n: max(n, 1)
    x1, y1, z1, b1 = one(nx - 1), one(ny - 1), one(nz - 1), nb - 1
    dma = pltpu.SemaphoreType.DMA
    vmem = pl.BlockSpec(memory_space=pltpu.VMEM)
    hbm = pl.BlockSpec(memory_space=pl.ANY)
    scratch = [
        pltpu.VMEM((depth, width), BF16),
        pltpu.VMEM((depth, width), BF16),
        pltpu.VMEM((width, depth), BF16),
        pltpu.VMEM((nz, block, depth), BF16),
        pltpu.VMEM((nz, block, depth), BF16),
        pltpu.VMEM((depth, crops), BF16),
        pltpu.VMEM((crops, width), F32),
        pltpu.VMEM((crops, width), F32),
        pltpu.VMEM((crops, width), BF16),
        pltpu.VMEM((8, width), F32),
        pltpu.VMEM((ITERS, 1, width), F32),
        pltpu.VMEM((ITERS, 2 * groups, LANES), F32),
        pltpu.VMEM((groups, LANES), F32),
        pltpu.VMEM((groups, LANES), F32),
        pltpu.VMEM((ITERS, b1, 1, width), F32),
        pltpu.VMEM((ITERS, x1, 2 * groups, LANES), F32),
        pltpu.VMEM((ITERS, 2 * groups, LANES), F32),
        pltpu.VMEM((ITERS, z1, 2 * groups, LANES), F32),
        pltpu.VMEM((nz, block, depth), BF16),
        pltpu.VMEM((x1, nz, rows, depth), BF16),
        pltpu.VMEM((nz, rows, depth), BF16),
        pltpu.VMEM((z1, rows, depth), BF16),
        pltpu.VMEM((2, ny, dr, width), F32),
        pltpu.VMEM((2, ny, dr, width), BF16),
        pltpu.VMEM((ny, dr, width), BF16),
        pltpu.VMEM((y1, dr, width), BF16),
        pltpu.VMEM((y1, dr, width), BF16),
        dma((2,)),
        dma((x1,)), dma((x1,)), dma((half,)), dma((half,)), dma((half,)), dma((half,)),
        dma((half,)), dma((half,)), dma((half,)), dma((half,)), dma((nz * x1,)), dma((nz * x1,)),
        dma((ITERS, b1)), dma((ITERS, b1)), dma((ITERS, x1)), dma((ITERS, x1)),
        dma((ITERS, z1)), dma((ITERS, z1)),
        dma((nz * x1,)), dma((nz * x1,)), dma((z1,)), dma((z1,)),
        dma((nch,)), dma((nch,)), dma((nch, y1)), dma((nch, y1)),
    ]
    return pl.pallas_call(
        functools.partial(kernel, nx, nz, ny),
        out_shape=(
            jax.ShapeDtypeStruct((dr, width), F32),
            jax.ShapeDtypeStruct((rows, depth), F32),
        ),
        in_specs=[vmem, vmem, hbm, hbm],
        out_specs=(vmem, vmem),
        scratch_shapes=scratch,
        compiler_params=pltpu.CompilerParams(
            collective_id=0, has_side_effects=True, vmem_limit_bytes=60 * 1024 * 1024
        ),
        cost_estimate=pl.CostEstimate(
            flops=8 * crops * width * depth, bytes_accessed=4 * depth * width,
            transcendentals=2 * crops * width,
        ),
    )(student_feats, teacher_feats, student_protos, teacher_protos)


def solution(mesh, nz=8):
    nx, ny = mesh.shape["proto"] // nz, mesh.shape["batch"] // 2
    in_specs = (
        P(("batch", "proto"), None),
        P(("batch", "proto"), None),
        P(None, "proto"),
        P(None, "proto"),
    )
    out_specs = (P("batch", "proto"), P(("batch", "proto"), None))
    return jax.shard_map(
        functools.partial(shards, nx, nz, ny),
        mesh=mesh, in_specs=in_specs, out_specs=out_specs, check_vma=False,
    )
```

time: 737 us -> 109 us (0.15); the launches traced: 726 us -> 108 us
  blocking collectives: 299 us -> 0 us
  waiting for transfers between devices: 274 us -> 0 us
  matrix products: 110 us -> 0 us
  Pallas kernels: 0 us -> 105 us
  other arithmetic: 19.4 us -> 0 us
  between operations: 14.2 us -> 0.65 us
    psum x6 -> x0, blocking collectives: 299 us -> none  [the longest x3 228 us: shards(): crop_sum = lax.psum(crop_local, 'proto')]
    psum x1 -> x0, waiting for transfers between devices: 161 us -> none  [shards(): total_grad = lax.psum(partial_grad, 'proto')]
    dot_general x10 -> x0, matrix products: 110 us -> none  [the longest x3 48 us: shards(): jnp.dot(crop_scale, masses, precision=lax.Precision.HIGHEST)]
    pallas_call x0 -> x1, Pallas kernels: none -> 105 us  [shards(): pl.pallas_call(functools.partial(kernel, nx, nz, ny), out_shape=(jax.Shap...]
    all_gather x2 -> x0, waiting for transfers between devices: 77.5 us -> none  [the longest x1 77.5 us: shards(): lax.all_gather(teacher_feats, 'proto', axis=0, tiled=True)]
    reduce_scatter x1 -> x0, waiting for transfers between devices: 34.4 us -> none  [shards(): lax.psum_scatter(lax.dot_general(stud_half, grad_half, (((0,), (0,)), (()...]
    convert_element_type x1 -> x0, other arithmetic: 12.4 us -> none  [shards(): grad_half = (probs - targets).astype(jnp.bfloat16)]
  transfers between devices with their start and end apart: 4 -> 0, of which waited for: 3 -> 0; matrix products, arithmetic and copies ran while one was open for 14% -> 0% of each run, Pallas kernels for 0% -> 0%
where the time goes in v1:
time: 109 us; the launch traced here: 108 us
  Pallas kernels  105 us (96%)
  local copies, waits for them, and re-layouts  2.34 us (2%)
    pallas_call x1, Pallas kernels, shards(): pl.pallas_call(functools.partial(kernel, nx, nz, ny), out_shape=(jax.Shap...  105 us
    unnamed x4, local copies, waits for them, and re-layouts  2.34 us

profile of v1, /device:TPU:1, one launch (start us, length us, event | category | flops | bytes accessed | tf_op | source)
XLA Modules:
  0.0 108.3 jit_solution(2971555688981367135)
XLA Ops:
  0.6 105.3 %shard_map.59 = (f32[32,2048]{1,0:T(8,128)}, f32[64,256]{1,0:T(8,128)}) custom-call(bf16[64,256]{1,0:T(8,128)(2,1)} %sf.1, bf16[64,256]{1,0:T(8,128)(2,1)} %tf.1, bf16[256,2048]{1,0:T(8,128)(2,1)} %sp_hbm.1, bf16[256,2048]{1,0:T(8,128)(2,1)} %tp_hbm.1), custom_call_target="tpu_custom_call" | custom-call | flops 8589934592 | bytes 2097152 | tf_op jit(solution)/shard_map/pallas_call | solution.py:504
  105.9 0.0 copy-start
  105.9 1.7 %copy.8 = f32[32,2048]{1,0:T(8,128)} copy(f32[32,2048]{1,0:T(8,128)} %get-tuple-element.4) | data formatting | bytes 524288
  107.6 0.0 copy-done
  107.6 0.6 copy.9
Async XLA Ops:
  105.9 1.7 %copy-start = (f32[64,256]{1,0:T(8,128)S(1)}, f32[64,256]{1,0:T(8,128)}, u32[]{:S(2)}) copy-start(f32[64,256]{1,0:T(8,128)} %get-tuple-element.5) | copy-start | bytes 196612

commit v2 on v1

v2 whole, which is shorter than its diff:
```python
import functools

import jax
import jax.numpy as jnp
from jax import lax
from jax.experimental import pallas as pl
from jax.experimental.pallas import tpu as pltpu
from jax.sharding import PartitionSpec as P

ITERS = 3
STUDENT_TEMP = 0.1
TEACHER_TEMP = 0.07
LOG2E = 1.4426950408889634
MESH = pl.DeviceIdType.MESH
F32 = jnp.float32
BF16 = jnp.bfloat16
LANES = 128


def unit_rows(feats):
    values = feats.astype(F32)
    norm = jnp.sqrt(jnp.sum(values * values, axis=1, keepdims=True) + 1e-06)
    return values / norm, norm


def kernel(
    nx, nz, ny,
    sf, tf, sp_hbm, tp_hbm,
    pg_out, fg_out,
    tp, sp, spt, tall, uall, ut, m, e, g,
    colacc, ps, lse_acc, pay, cinv, ccs,
    cb, pb,
    ugb, ug0, near, xr, zs, zr,
    pgf, pgb, cr, ys, yr,
    local_s,
    tz_s, tz_r, tx_s, tx_r, uz_s, uz_r, ux_s, ux_r,
    cb_s, cb_r, pb_s, pb_r,
    fn_s, fn_r, fx_s, fx_r, fz_s, fz_r, pc_s, pc_r, py_s, py_r,
):
    rows = sf.shape[0]
    depth, width = tp.shape
    block = nx * rows
    crops = nz * block
    nb = 2 * ny
    dr = depth // nb
    tile = min(256, width)
    groups = crops // LANES
    per = block // LANES
    chunk = min(512, width)

    pid = lax.axis_index("proto")
    bid = lax.axis_index("batch")
    x, z = pid // nz, pid % nz
    y, c = bid // 2, bid % 2
    my = pl.multiple_of(x * rows, rows)

    def to_xz(xx, zz):
        return {"proto": (xx % nx) * nz + zz % nz}

    def to_b(bb):
        return {"batch": bb % nb}

    def remote(src, dst, ss, rs, dev):
        return pltpu.make_async_remote_copy(
            src_ref=src, dst_ref=dst, send_sem=ss, recv_sem=rs, device_id=dev, device_id_type=MESH
        )

    drain = []

    barrier = pltpu.get_barrier_semaphore()
    for kx in range(nx):
        for kz in range(nz):
            if kx or kz:
                pl.semaphore_signal(
                    barrier, inc=1, device_id=to_xz(x + kx, z + kz), device_id_type=MESH
                )
    for k in range(1, nb):
        pl.semaphore_signal(barrier, inc=1, device_id=to_b(bid + k), device_id_type=MESH)

    load_tp = pltpu.make_async_copy(tp_hbm, tp, local_s.at[0])
    load_sp = pltpu.make_async_copy(sp_hbm, sp, local_s.at[1])
    load_tp.start()
    load_sp.start()

    tall[z, pl.ds(my, rows), :] = unit_rows(tf[...])[0].astype(BF16)
    uall[z, pl.ds(my, rows), :] = unit_rows(sf[...])[0].astype(BF16)
    colacc[...] = jnp.zeros_like(colacc)
    eye = lax.broadcasted_iota(jnp.int32, (LANES, LANES), 0) == lax.broadcasted_iota(
        jnp.int32, (LANES, LANES), 1
    )

    def to_row(col):
        return jnp.sum(jnp.where(eye, col, 0.0), axis=0, keepdims=True)

    def to_col(row):
        return jnp.sum(jnp.where(eye, row, 0.0), axis=1, keepdims=True)

    pl.semaphore_wait(barrier, (nx * nz - 1) + (nb - 1))

    near_z = sorted({1, nz - 1})
    far_z = [d for d in range(1, nz) if d not in near_z]
    far_z = sorted(far_z, key=lambda d: (min(d, nz - d), d))

    def tz(d):
        ref = tall.at[z, pl.ds(my, rows)]
        return remote(ref, ref, tz_s.at[d], tz_r.at[d], to_xz(x, z + d))

    def trow(d):
        ref = tall.at[z]
        return remote(ref, ref, tz_s.at[d], tz_r.at[d], to_xz(x, z + d))

    def tx(d, k):
        ref = tall.at[(z + nz - d) % nz, pl.ds(my, rows)]
        i = d * (nx - 1) + k - 1
        return remote(ref, ref, tx_s.at[i], tx_r.at[i], to_xz(x + k, z))

    def uz(d):
        ref = uall.at[z, pl.ds(my, rows)]
        return remote(ref, ref, uz_s.at[d], uz_r.at[d], to_xz(x, z + d))

    def ux(d, k):
        ref = uall.at[(z + nz - d) % nz, pl.ds(my, rows)]
        i = d * (nx - 1) + k - 1
        return remote(ref, ref, ux_s.at[i], ux_r.at[i], to_xz(x + k, z))

    for k in range(1, nx):
        tx(0, k).start()
    for d in far_z:
        tz(d).start()

    def compute_m(blk):
        row0 = pl.multiple_of(blk * block, block)
        a = tall[blk]
        for j in range(width // tile):
            cols = slice(j * tile, (j + 1) * tile)
            s = jnp.dot(a, tp[:, cols], preferred_element_type=F32)
            v = jnp.exp2(s * (LOG2E / TEACHER_TEMP))
            m[pl.ds(row0, block), cols] = v
            colacc[:, cols] += jnp.sum(v.reshape(block // 8, 8, tile), axis=0)

    for k in range(1, nx):
        tx(0, k).wait_recv()
    for d in near_z:
        trow(d).start()
    load_tp.wait()
    compute_m(z)
    for d in far_z:
        tz(d).wait_recv()
        for k in range(1, nx):
            tx(d, k).start()
    for k in range(1, nx):
        ux(0, k).start()
    for d in range(1, nz):
        uz(d).start()

    def pick(s, table):
        out = jnp.int32(table[0])
        for i in range(1, len(table)):
            out = jnp.where(s == i, table[i], out)
        return out

    arrivals = far_z[:2] + near_z + far_z[2:]

    @pl.loop(0, nz - 1)
    def _(s):
        d = pick(s, arrivals)
        is_near = (d == 1) | (d == nz - 1)

        @pl.when(is_near)
        def _():
            trow(d).wait_recv()

        @pl.when(jnp.logical_not(is_near))
        def _():
            for k in range(1, nx):
                tx(d, k).wait_recv()

        compute_m((z + nz - d) % nz)

    def gathered():
        for k in range(1, nx):
            tx(0, k).wait_send()
        for d in near_z:
            trow(d).wait_send()
        for d in far_z:
            tz(d).wait_send()
            for k in range(1, nx):
                tx(d, k).wait_send()

    drain.append(gathered)

    def cb_copy(it, k):
        return remote(
            ps.at[it], cb.at[it, k - 1], cb_s.at[it, k - 1], cb_r.at[it, k - 1], to_b(bid + k)
        )

    def pb_copy(it, kx, kz):
        i = kx * nz + kz - 1
        return remote(
            pay.at[it], pb.at[it, i], pb_s.at[it, i], pb_r.at[it, i], to_xz(x + kx, z + kz)
        )

    others = [(kx, kz) for kx in range(nx) for kz in range(nz) if kx or kz]

    def pb_total(it):
        total = pay[it].astype(F32)
        for i in range(nx * nz - 1):
            total = total + pb[it, i].astype(F32)
        return total

    def compute_e(blk):
        row0 = pl.multiple_of(blk * block, block)
        a = uall[blk]
        acc = jnp.zeros((block, LANES), F32)
        for j in range(width // tile):
            cols = slice(j * tile, (j + 1) * tile)
            s = jnp.dot(a, sp[:, cols], preferred_element_type=F32)
            v = jnp.exp2(jnp.minimum(s * (LOG2E / STUDENT_TEMP) - 2.0, 127.0))
            e[pl.ds(row0, block), cols] = v
            for t in range(tile // LANES):
                acc += v[:, t * LANES : (t + 1) * LANES]
        for i in range(per):
            col = jnp.sum(acc[i * LANES : (i + 1) * LANES], axis=1, keepdims=True)
            lse_acc[pl.ds(blk * per + i, 1), :] = to_row(col)

    def e_blocks(ds):
        @pl.loop(0, len(ds))
        def _(s):
            d = pick(s, ds)
            for k in range(1, nx):
                ux(d, k).wait_recv()
            compute_e((z + nz - d) % nz)

    def u_forward(ds):
        for d in ds:
            uz(d).wait_recv()
            for k in range(1, nx):
                ux(d, k).start()

    def colsum():
        def body(i, acc):
            col = to_col(ccs[pl.ds(i, 1), :])
            for q in range(LANES // 8):
                acc = acc + m[pl.ds(i * LANES + q * 8, 8), :] * col[q * 8 : (q + 1) * 8]
            return acc

        return lax.fori_loop(0, groups, body, jnp.zeros((8, width), F32), unroll=min(4, groups))

    def rowsum(scale):
        def body(i):
            acc = jnp.zeros((LANES, LANES), F32)
            for t in range(width // LANES):
                cols = slice(t * LANES, (t + 1) * LANES)
                acc = acc + m[pl.ds(i * LANES, LANES), cols] * scale[:, cols]
            ccs[pl.ds(i, 1), :] = to_row(jnp.sum(acc, axis=1, keepdims=True))

        pl.loop(0, groups, unroll=min(4, groups))(body)

    u_order = [d for d in range(1, nz)]
    cut = (len(u_order) - 1) // 2
    for it in range(ITERS):
        part = colacc[...] if it == 0 else colsum()
        ps[it] = jnp.sum(part, axis=0, keepdims=True)
        for k in range(1, nb):
            cb_copy(it, k).start()
        if it == 0:
            load_sp.wait()

            @pl.loop(0, width // tile)
            def _(j):
                cols = pl.ds(pl.multiple_of(j * tile, tile), tile)
                spt[cols, :] = sp[:, cols].T

        elif it == 1:
            u_forward(u_order[cut:])
            e_blocks(u_order[:cut])
        else:
            pay[ITERS] = lse_acc[...].astype(BF16)
            for kx, kz in others:
                pb_copy(ITERS, kx, kz).start()

            @pl.loop(0, nz)
            def _(k):
                ut[:, pl.ds(pl.multiple_of(k * block, block), block)] = uall[k].T

        for k in range(1, nb):
            cb_copy(it, k).wait_recv()
        total = ps[it]
        for k in range(1, nb):
            total = total + cb[it, k - 1]
        scale = 1.0 / total
        if it == 0:
            u_forward(u_order[:cut])
        rowsum(scale)
        if it == ITERS - 1:
            cps = scale
        pay[it] = ccs[...].astype(BF16)
        for kx, kz in others:
            pb_copy(it, kx, kz).start()
        if it == 0:
            e_blocks([0])
        elif it == 1:
            e_blocks(u_order[cut:])
        else:
            for kx, kz in others:
                pb_copy(ITERS, kx, kz).wait_recv()
            cinv[...] = 1.0 / pb_total(ITERS)
        for kx, kz in others:
            pb_copy(it, kx, kz).wait_recv()
        ccs[...] = 1.0 / pb_total(it)

        def reduced(it=it):
            for k in range(1, nb):
                cb_copy(it, k).wait_send()
            for kx, kz in others:
                pb_copy(it, kx, kz).wait_send()

        drain.append(reduced)

    def student():
        for k in range(1, nx):
            ux(0, k).wait_send()
        for d in range(1, nz):
            uz(d).wait_send()
            for k in range(1, nx):
                ux(d, k).wait_send()
        for kx, kz in others:
            pb_copy(ITERS, kx, kz).wait_send()

    drain.append(student)

    def fn_copy(d):
        i = near_z.index(d)
        return remote(
            ugb.at[(z + d) % nz], near.at[i], fn_s.at[i], fn_r.at[i], to_xz(x, z + d)
        )

    def fx_copy(d, k):
        xx = (x + k) % nx
        i = d * (nx - 1) + k - 1
        return remote(
            ugb.at[(z + d) % nz, pl.ds(pl.multiple_of(xx * rows, rows), rows)],
            xr.at[k - 1, d], fx_s.at[i], fx_r.at[i], to_xz(xx, z),
        )

    def fz_copy(d):
        return remote(zs.at[d], zr.at[d], fz_s.at[d], fz_r.at[d], to_xz(x, z + d))

    late = far_z[::-1]
    series = near_z + late + [0]
    pairs = [series[i : i + 2] for i in range(0, nz, 2)]

    @pl.loop(0, len(pairs))
    def _(s):
        blks = [(z + pick(s, [p[i] for p in pairs])) % nz for i in range(2)]
        invs, scas = [
            [
                jnp.concatenate([to_col(ref[pl.ds(blk * per + i, 1), :]) for i in range(per)], axis=0)
                for blk in blks
            ]
            for ref in (cinv, ccs)
        ]
        acc = jnp.zeros((2 * block, depth), F32)
        for j in range(width // tile):
            cols = slice(j * tile, (j + 1) * tile)
            both = []
            for blk, inv, sca in zip(blks, invs, scas):
                at = pl.ds(pl.multiple_of(blk * block, block), block)
                prob = e[at, cols] * inv
                target = (m[at, cols] * sca) * cps[:, cols]
                gh = (prob - target).astype(BF16)
                g[at, cols] = gh
                both.append(gh)
            acc += jnp.dot(jnp.concatenate(both, axis=0), spt[cols, :], preferred_element_type=F32)
        for i, blk in enumerate(blks):
            ugb[blk] = acc[i * block : (i + 1) * block].astype(BF16)

        @pl.when(s == len(pairs) - 1)
        def _():
            ug0[...] = acc[block:]

        for i, p in enumerate(pairs):

            @pl.when(s == i)
            def _():
                for d in p:
                    if d in near_z:
                        fn_copy(d).start()
                    elif d:
                        for k in range(1, nx):
                            fx_copy(d, k).start()

    nch = width // chunk

    def pc_copy(j):
        cols = pl.ds(pl.multiple_of(j * chunk, chunk), chunk)
        return remote(
            pgb.at[1 - c, :, :, cols], cr.at[:, :, cols], pc_s.at[j], pc_r.at[j], to_b(y * 2 + 1 - c)
        )

    def py_copy(j, k):
        cols = pl.ds(pl.multiple_of(j * chunk, chunk), chunk)
        return remote(
            ys.at[k - 1, :, cols], yr.at[k - 1, :, cols],
            py_s.at[j, k - 1], py_r.at[j, k - 1], to_b(bid + 2 * k),
        )

    def pc_sum(j):
        cols = pl.ds(pl.multiple_of(j * chunk, chunk), chunk)
        pc_copy(j).wait_recv()
        for k in range(1, ny):
            yy = (y + k) % ny
            ys[k - 1, :, cols] = (pgf[c, yy, :, cols] + cr[yy, :, cols].astype(F32)).astype(BF16)
            py_copy(j, k).start()
        pg_out[:, cols] = pgf[c, y, :, cols] + cr[y, :, cols].astype(F32)

    @pl.loop(0, nch)
    def _(j):
        cols = pl.ds(pl.multiple_of(j * chunk, chunk), chunk)
        part = jnp.dot(ut[...], g[:, cols], preferred_element_type=F32)
        for yy in range(ny):
            for cc in range(2):
                d0 = (yy * 2 + cc) * dr
                pgf[cc, yy, :, cols] = part[d0 : d0 + dr]
                pgb[cc, yy, :, cols] = part[d0 : d0 + dr].astype(BF16)
        pc_copy(j).start()

        @pl.when(j > 0)
        def _():
            pc_sum(j - 1)

        @pl.when(j == min(1, nch - 1))
        def _():
            total = ug0[...]
            for i, d in enumerate(near_z):
                fn_copy(d).wait_recv()
                total = total + near[i].astype(F32)
            ug0[...] = total
            ugb[z] = total.astype(BF16)
            for k in range(1, nx):
                fx_copy(0, k).start()

    def x_sum(d):
        for k in range(1, nx):
            fx_copy(d, k).wait_recv()
        total = ugb[(z + d) % nz, pl.ds(my, rows), :].astype(F32) if d else ug0[pl.ds(my, rows), :]
        for k in range(1, nx):
            total = total + xr[k - 1, d].astype(F32)
        return total

    for i, d in enumerate(late):
        zs[d] = x_sum(d).astype(BF16)
        fz_copy(d).start()
        if i == 0:
            pc_sum(nch - 1)
    if not late:
        pc_sum(nch - 1)
    total = x_sum(0)
    for d in late:
        fz_copy(d).wait_recv()
        total = total + zr[d].astype(F32)
    total = total / STUDENT_TEMP
    unit, norm = unit_rows(sf[...])
    inner = jnp.sum(unit * total, axis=1, keepdims=True)
    fg_out[...] = (total - unit * inner) / norm

    @pl.loop(0, nch)
    def _(j):
        cols = pl.ds(pl.multiple_of(j * chunk, chunk), chunk)
        total = pg_out[:, cols]
        for k in range(1, ny):
            py_copy(j, k).wait_recv()
            total = total + yr[k - 1, :, cols].astype(F32)
        pg_out[:, cols] = total / STUDENT_TEMP

    def grads():
        for d in near_z:
            fn_copy(d).wait_send()
        for d in late + [0]:
            for k in range(1, nx):
                fx_copy(d, k).wait_send()
        for d in late:
            fz_copy(d).wait_send()

        @pl.loop(0, nch)
        def _(j):
            pc_copy(j).wait_send()
            for k in range(1, ny):
                py_copy(j, k).wait_send()

    drain.append(grads)
    for leave in drain:
        leave()


def shards(nx, nz, ny, student_feats, teacher_feats, student_protos, teacher_protos):
    rows, depth = student_feats.shape
    width = student_protos.shape[1]
    block, nb = nx * rows, 2 * ny
    crops, dr = nz * block, depth // nb
    groups = crops // LANES
    chunk = min(512, width)
    nch = width // chunk
    one = lambda n: max(n, 1)
    x1, y1, b1 = one(nx - 1), one(ny - 1), nb - 1
    dma = pltpu.SemaphoreType.DMA
    vmem = pl.BlockSpec(memory_space=pltpu.VMEM)
    hbm = pl.BlockSpec(memory_space=pl.ANY)
    scratch = [
        pltpu.VMEM((depth, width), BF16),
        pltpu.VMEM((depth, width), BF16),
        pltpu.VMEM((width, depth), BF16),
        pltpu.VMEM((nz, block, depth), BF16),
        pltpu.VMEM((nz, block, depth), BF16),
        pltpu.VMEM((depth, crops), BF16),
        pltpu.VMEM((crops, width), F32),
        pltpu.VMEM((crops, width), F32),
        pltpu.VMEM((crops, width), BF16),
        pltpu.VMEM((8, width), F32),
        pltpu.VMEM((ITERS, 1, width), F32),
        pltpu.VMEM((groups, LANES), F32),
        pltpu.VMEM((ITERS + 1, groups, LANES), BF16),
        pltpu.VMEM((groups, LANES), F32),
        pltpu.VMEM((groups, LANES), F32),
        pltpu.VMEM((ITERS, b1, 1, width), F32),
        pltpu.VMEM((ITERS + 1, nx * nz - 1, groups, LANES), BF16),
        pltpu.VMEM((nz, block, depth), BF16),
        pltpu.VMEM((block, depth), F32),
        pltpu.VMEM((2, block, depth), BF16),
        pltpu.VMEM((x1, nz, rows, depth), BF16),
        pltpu.VMEM((nz, rows, depth), BF16),
        pltpu.VMEM((nz, rows, depth), BF16),
        pltpu.VMEM((2, ny, dr, width), F32),
        pltpu.VMEM((2, ny, dr, width), BF16),
        pltpu.VMEM((ny, dr, width), BF16),
        pltpu.VMEM((y1, dr, width), BF16),
        pltpu.VMEM((y1, dr, width), BF16),
        dma((2,)),
        dma((nz,)), dma((nz,)), dma((nz * x1,)), dma((nz * x1,)),
        dma((nz,)), dma((nz,)), dma((nz * x1,)), dma((nz * x1,)),
        dma((ITERS, b1)), dma((ITERS, b1)),
        dma((ITERS + 1, nx * nz - 1)), dma((ITERS + 1, nx * nz - 1)),
        dma((2,)), dma((2,)), dma((nz * x1,)), dma((nz * x1,)), dma((nz,)), dma((nz,)),
        dma((nch,)), dma((nch,)), dma((nch, y1)), dma((nch, y1)),
    ]
    return pl.pallas_call(
        functools.partial(kernel, nx, nz, ny),
        out_shape=(
            jax.ShapeDtypeStruct((dr, width), F32),
            jax.ShapeDtypeStruct((rows, depth), F32),
        ),
        in_specs=[vmem, vmem, hbm, hbm],
        out_specs=(vmem, vmem),
        scratch_shapes=scratch,
        compiler_params=pltpu.CompilerParams(
            collective_id=0, has_side_effects=True, vmem_limit_bytes=60 * 1024 * 1024
        ),
        cost_estimate=pl.CostEstimate(
            flops=8 * crops * width * depth, bytes_accessed=4 * depth * width,
            transcendentals=2 * crops * width,
        ),
    )(student_feats, teacher_feats, student_protos, teacher_protos)


def solution(mesh, nz=8):
    nx, ny = mesh.shape["proto"] // nz, mesh.shape["batch"] // 2
    in_specs = (
        P(("batch", "proto"), None),
        P(("batch", "proto"), None),
        P(None, "proto"),
        P(None, "proto"),
    )
    out_specs = (P("batch", "proto"), P(("batch", "proto"), None))
    return jax.shard_map(
        functools.partial(shards, nx, nz, ny),
        mesh=mesh, in_specs=in_specs, out_specs=out_specs, check_vma=False,
    )
```

time: 109 us -> 95.9 us (0.88)
  Pallas kernels: 105 us -> 92.7 us
    pallas_call x1, Pallas kernels: 105 us -> 92.7 us  [shards(): pl.pallas_call(functools.partial(kernel, nx, nz, ny), out_shape=(jax.Shap...]
where the time goes in v2:
time: 95.9 us; the launch traced here: 95.7 us
  Pallas kernels  92.7 us (97%)
  local copies, waits for them, and re-layouts  2.34 us (2%)
    pallas_call x1, Pallas kernels, shards(): pl.pallas_call(functools.partial(kernel, nx, nz, ny), out_shape=(jax.Shap...  92.7 us
    unnamed x4, local copies, waits for them, and re-layouts  2.34 us

profile of v2, /device:TPU:1, one launch (start us, length us, event | category | flops | bytes accessed | tf_op | source)
XLA Modules:
  0.0 95.7 jit_solution(12082882860471475162)
XLA Ops:
  0.6 92.7 %shard_map.59 = (f32[32,2048]{1,0:T(8,128)}, f32[64,256]{1,0:T(8,128)}) custom-call(bf16[64,256]{1,0:T(8,128)(2,1)} %sf.1, bf16[64,256]{1,0:T(8,128)(2,1)} %tf.1, bf16[256,2048]{1,0:T(8,128)(2,1)} %sp_hbm.1, bf16[256,2048]{1,0:T(8,128)(2,1)} %tp_hbm.1), custom_call_target="tpu_custom_call" | custom-call | flops 8589934592 | bytes 2097152 | tf_op jit(solution)/shard_map/pallas_call | solution.py:546
  93.4 0.0 copy-start
  93.4 1.7 %copy.8 = f32[32,2048]{1,0:T(8,128)} copy(f32[32,2048]{1,0:T(8,128)} %get-tuple-element.4) | data formatting | bytes 524288
  95.1 0.0 copy-done
  95.1 0.6 copy.9
Async XLA Ops:
  93.4 1.7 %copy-start = (f32[64,256]{1,0:T(8,128)S(1)}, f32[64,256]{1,0:T(8,128)}, u32[]{:S(2)}) copy-start(f32[64,256]{1,0:T(8,128)} %get-tuple-element.5) | copy-start | bytes 196612

commit v3 on v2

--- a/solution.py
+++ b/solution.py
@@ -33,9 +33,9 @@
     ugb, ug0, near, xr, zs, zr,
     pgf, pgb, cr, ys, yr,
     local_s,
-    tz_s, tz_r, tx_s, tx_r, uz_s, uz_r, ux_s, ux_r,
-    cb_s, cb_r, pb_s, pb_r,
-    fn_s, fn_r, fx_s, fx_r, fz_s, fz_r, pc_s, pc_r, py_s, py_r,
+    tz_r, tx_r, uz_r, ux_r, cb_r, pb_r, fn_r, fx_r, fz_r, pc_r, py_r,
+    t_s, u_s, cb_s, pb_s, f_s, p_s,
+    spare,
 ):
     rows = sf.shape[0]
     depth, width = tp.shape
@@ -67,13 +67,23 @@
 
     drain = []
 
+    row_bytes = rows * depth * 2
+
+    def landed(sem, count):
+        if count:
+            ref = spare.at[pl.ds(0, count)]
+            remote(ref, ref, sem, sem, to_xz(x, z + 1)).wait_recv()
+
+    def gone(sem, count):
+        if count:
+            ref = spare.at[pl.ds(0, count)]
+            remote(ref, ref, sem, sem, to_xz(x, z + 1)).wait_send()
+
     barrier = pltpu.get_barrier_semaphore()
-    for kx in range(nx):
-        for kz in range(nz):
-            if kx or kz:
-                pl.semaphore_signal(
-                    barrier, inc=1, device_id=to_xz(x + kx, z + kz), device_id_type=MESH
-                )
+    for k in range(1, nx):
+        pl.semaphore_signal(barrier, inc=1, device_id=to_xz(x + k, z), device_id_type=MESH)
+    for k in range(1, nz):
+        pl.semaphore_signal(barrier, inc=1, device_id=to_xz(x, z + k), device_id_type=MESH)
     for k in range(1, nb):
         pl.semaphore_signal(barrier, inc=1, device_id=to_b(bid + k), device_id_type=MESH)
 
@@ -95,33 +105,35 @@
     def to_col(row):
         return jnp.sum(jnp.where(eye, row, 0.0), axis=1, keepdims=True)
 
-    pl.semaphore_wait(barrier, (nx * nz - 1) + (nb - 1))
+    pl.semaphore_wait(barrier, (nx - 1) + (nz - 1) + (nb - 1))
 
     near_z = sorted({1, nz - 1})
     far_z = [d for d in range(1, nz) if d not in near_z]
     far_z = sorted(far_z, key=lambda d: (min(d, nz - d), d))
 
+    u_order = [d for d in range(1, nz)]
+    cut = (len(u_order) - 1) // 2
+    u_first, u_second = u_order[:cut], u_order[cut:]
+
     def tz(d):
         ref = tall.at[z, pl.ds(my, rows)]
-        return remote(ref, ref, tz_s.at[d], tz_r.at[d], to_xz(x, z + d))
+        return remote(ref, ref, t_s, tz_r.at[d], to_xz(x, z + d))
 
     def trow(d):
         ref = tall.at[z]
-        return remote(ref, ref, tz_s.at[d], tz_r.at[d], to_xz(x, z + d))
+        return remote(ref, ref, t_s, tz_r.at[d], to_xz(x, z + d))
 
     def tx(d, k):
         ref = tall.at[(z + nz - d) % nz, pl.ds(my, rows)]
-        i = d * (nx - 1) + k - 1
-        return remote(ref, ref, tx_s.at[i], tx_r.at[i], to_xz(x + k, z))
+        return remote(ref, ref, t_s, tx_r.at[d], to_xz(x + k, z))
 
     def uz(d):
         ref = uall.at[z, pl.ds(my, rows)]
-        return remote(ref, ref, uz_s.at[d], uz_r.at[d], to_xz(x, z + d))
+        return remote(ref, ref, u_s, uz_r.at[0 if d in u_first else 1], to_xz(x, z + d))
 
     def ux(d, k):
         ref = uall.at[(z + nz - d) % nz, pl.ds(my, rows)]
-        i = d * (nx - 1) + k - 1
-        return remote(ref, ref, ux_s.at[i], ux_r.at[i], to_xz(x + k, z))
+        return remote(ref, ref, u_s, ux_r.at[d], to_xz(x + k, z))
 
     for k in range(1, nx):
         tx(0, k).start()
@@ -138,8 +150,7 @@
             m[pl.ds(row0, block), cols] = v
             colacc[:, cols] += jnp.sum(v.reshape(block // 8, 8, tile), axis=0)
 
-    for k in range(1, nx):
-        tx(0, k).wait_recv()
+    landed(tx_r.at[0], nx - 1)
     for d in near_z:
         trow(d).start()
     load_tp.wait()
@@ -172,35 +183,27 @@
 
         @pl.when(jnp.logical_not(is_near))
         def _():
-            for k in range(1, nx):
-                tx(d, k).wait_recv()
+            landed(tx_r.at[d], nx - 1)
 
         compute_m((z + nz - d) % nz)
 
-    def gathered():
-        for k in range(1, nx):
-            tx(0, k).wait_send()
-        for d in near_z:
-            trow(d).wait_send()
-        for d in far_z:
-            tz(d).wait_send()
-            for k in range(1, nx):
-                tx(d, k).wait_send()
-
-    drain.append(gathered)
+    drain.append(lambda: gone(t_s, (nx - 1) * (1 + len(far_z)) + len(far_z) + nx * len(near_z)))
 
     def cb_copy(it, k):
         return remote(
-            ps.at[it], cb.at[it, k - 1], cb_s.at[it, k - 1], cb_r.at[it, k - 1], to_b(bid + k)
+            ps.at[it], cb.at[it, k - 1], cb_s, cb_r.at[it], to_b(bid + k)
         )
 
     def pb_copy(it, kx, kz):
         i = kx * nz + kz - 1
         return remote(
-            pay.at[it], pb.at[it, i], pb_s.at[it, i], pb_r.at[it, i], to_xz(x + kx, z + kz)
+            pay.at[it], pb.at[it, i], pb_s, pb_r.at[it], to_xz(x + kx, z + kz)
         )
 
     others = [(kx, kz) for kx in range(nx) for kz in range(nz) if kx or kz]
+
+    def pb_landed(it):
+        remote(pb.at[it], pb.at[it], pb_s, pb_r.at[it], to_xz(x, z + 1)).wait_recv()
 
     def pb_total(it):
         total = pay[it].astype(F32)
@@ -227,13 +230,12 @@
         @pl.loop(0, len(ds))
         def _(s):
             d = pick(s, ds)
-            for k in range(1, nx):
-                ux(d, k).wait_recv()
+            landed(ux_r.at[d], nx - 1)
             compute_e((z + nz - d) % nz)
 
-    def u_forward(ds):
+    def u_forward(ds, i):
+        landed(uz_r.at[i], len(ds))
         for d in ds:
-            uz(d).wait_recv()
             for k in range(1, nx):
                 ux(d, k).start()
 
@@ -256,8 +258,6 @@
 
         pl.loop(0, groups, unroll=min(4, groups))(body)
 
-    u_order = [d for d in range(1, nz)]
-    cut = (len(u_order) - 1) // 2
     for it in range(ITERS):
         part = colacc[...] if it == 0 else colsum()
         ps[it] = jnp.sum(part, axis=0, keepdims=True)
@@ -272,8 +272,8 @@
                 spt[cols, :] = sp[:, cols].T
 
         elif it == 1:
-            u_forward(u_order[cut:])
-            e_blocks(u_order[:cut])
+            u_forward(u_second, 1)
+            e_blocks(u_first)
         else:
             pay[ITERS] = lse_acc[...].astype(BF16)
             for kx, kz in others:
@@ -283,14 +283,13 @@
             def _(k):
                 ut[:, pl.ds(pl.multiple_of(k * block, block), block)] = uall[k].T
 
-        for k in range(1, nb):
-            cb_copy(it, k).wait_recv()
+        remote(cb.at[it], cb.at[it], cb_s, cb_r.at[it], to_b(bid + 1)).wait_recv()
         total = ps[it]
         for k in range(1, nb):
             total = total + cb[it, k - 1]
         scale = 1.0 / total
         if it == 0:
-            u_forward(u_order[:cut])
+            u_forward(u_first, 0)
         rowsum(scale)
         if it == ITERS - 1:
             cps = scale
@@ -300,51 +299,33 @@
         if it == 0:
             e_blocks([0])
         elif it == 1:
-            e_blocks(u_order[cut:])
+            e_blocks(u_second)
         else:
-            for kx, kz in others:
-                pb_copy(ITERS, kx, kz).wait_recv()
+            pb_landed(ITERS)
             cinv[...] = 1.0 / pb_total(ITERS)
-        for kx, kz in others:
-            pb_copy(it, kx, kz).wait_recv()
+        pb_landed(it)
         ccs[...] = 1.0 / pb_total(it)
 
-        def reduced(it=it):
-            for k in range(1, nb):
-                cb_copy(it, k).wait_send()
-            for kx, kz in others:
-                pb_copy(it, kx, kz).wait_send()
-
-        drain.append(reduced)
-
-    def student():
-        for k in range(1, nx):
-            ux(0, k).wait_send()
-        for d in range(1, nz):
-            uz(d).wait_send()
-            for k in range(1, nx):
-                ux(d, k).wait_send()
-        for kx, kz in others:
-            pb_copy(ITERS, kx, kz).wait_send()
-
-    drain.append(student)
+
+    drain.append(lambda: gone(u_s, (nx - 1) * nz + nz - 1))
+    drain.append(lambda: remote(cb, cb, cb_s, cb_r.at[0], to_b(bid + 1)).wait_send())
+    drain.append(lambda: remote(pb, pb, pb_s, pb_r.at[0], to_xz(x, z + 1)).wait_send())
 
     def fn_copy(d):
         i = near_z.index(d)
         return remote(
-            ugb.at[(z + d) % nz], near.at[i], fn_s.at[i], fn_r.at[i], to_xz(x, z + d)
+            ugb.at[(z + d) % nz], near.at[i], f_s, fn_r.at[i], to_xz(x, z + d)
         )
 
     def fx_copy(d, k):
         xx = (x + k) % nx
-        i = d * (nx - 1) + k - 1
         return remote(
             ugb.at[(z + d) % nz, pl.ds(pl.multiple_of(xx * rows, rows), rows)],
-            xr.at[k - 1, d], fx_s.at[i], fx_r.at[i], to_xz(xx, z),
+            xr.at[k - 1, d], f_s, fx_r.at[d], to_xz(xx, z),
         )
 
     def fz_copy(d):
-        return remote(zs.at[d], zr.at[d], fz_s.at[d], fz_r.at[d], to_xz(x, z + d))
+        return remote(zs.at[d], zr.at[d], f_s, fz_r, to_xz(x, z + d))
 
     late = far_z[::-1]
     series = near_z + late + [0]
@@ -395,14 +376,14 @@
     def pc_copy(j):
         cols = pl.ds(pl.multiple_of(j * chunk, chunk), chunk)
         return remote(
-            pgb.at[1 - c, :, :, cols], cr.at[:, :, cols], pc_s.at[j], pc_r.at[j], to_b(y * 2 + 1 - c)
+            pgb.at[1 - c, :, :, cols], cr.at[:, :, cols], p_s, pc_r.at[j], to_b(y * 2 + 1 - c)
         )
 
     def py_copy(j, k):
         cols = pl.ds(pl.multiple_of(j * chunk, chunk), chunk)
         return remote(
             ys.at[k - 1, :, cols], yr.at[k - 1, :, cols],
-            py_s.at[j, k - 1], py_r.at[j, k - 1], to_b(bid + 2 * k),
+            p_s, py_r.at[j], to_b(bid + 2 * k),
         )
 
     def pc_sum(j):
@@ -413,6 +394,35 @@
             ys[k - 1, :, cols] = (pgf[c, yy, :, cols] + cr[yy, :, cols].astype(F32)).astype(BF16)
             py_copy(j, k).start()
         pg_out[:, cols] = pgf[c, y, :, cols] + cr[y, :, cols].astype(F32)
+
+    def x_sum(d):
+        landed(fx_r.at[d], nx - 1)
+        total = ugb[(z + d) % nz, pl.ds(my, rows), :].astype(F32) if d else ug0[pl.ds(my, rows), :]
+        for k in range(1, nx):
+            total = total + xr[k - 1, d].astype(F32)
+        return total
+
+    def z_send(d):
+        zs[d] = x_sum(d).astype(BF16)
+        fz_copy(d).start()
+
+    def own_rows():
+        total = ug0[...]
+        for i, d in enumerate(near_z):
+            fn_copy(d).wait_recv()
+            total = total + near[i].astype(F32)
+        ug0[...] = total
+        ugb[z] = total.astype(BF16)
+        for k in range(1, nx):
+            fx_copy(0, k).start()
+
+    after = {1: ["own"], 2: late[:2], 3: late[2:3]}
+    after = {j: a for j, a in after.items() if j < nch}
+    done = [d for a in after.values() for d in a]
+    rest = (["own"] if "own" not in done else []) + [d for d in late if d not in done]
+
+    def act(d):
+        own_rows() if d == "own" else z_send(d)
 
     @pl.loop(0, nch)
     def _(j):
@@ -429,35 +439,19 @@
         def _():
             pc_sum(j - 1)
 
-        @pl.when(j == min(1, nch - 1))
-        def _():
-            total = ug0[...]
-            for i, d in enumerate(near_z):
-                fn_copy(d).wait_recv()
-                total = total + near[i].astype(F32)
-            ug0[...] = total
-            ugb[z] = total.astype(BF16)
-            for k in range(1, nx):
-                fx_copy(0, k).start()
-
-    def x_sum(d):
-        for k in range(1, nx):
-            fx_copy(d, k).wait_recv()
-        total = ugb[(z + d) % nz, pl.ds(my, rows), :].astype(F32) if d else ug0[pl.ds(my, rows), :]
-        for k in range(1, nx):
-            total = total + xr[k - 1, d].astype(F32)
-        return total
-
-    for i, d in enumerate(late):
-        zs[d] = x_sum(d).astype(BF16)
-        fz_copy(d).start()
-        if i == 0:
-            pc_sum(nch - 1)
-    if not late:
-        pc_sum(nch - 1)
+        for jj, ds in after.items():
+
+            @pl.when(j == jj)
+            def _():
+                for d in ds:
+                    act(d)
+
+    pc_sum(nch - 1)
+    for d in rest:
+        act(d)
     total = x_sum(0)
+    landed(fz_r, len(late))
     for d in late:
-        fz_copy(d).wait_recv()
         total = total + zr[d].astype(F32)
     total = total / STUDENT_TEMP
     unit, norm = unit_rows(sf[...])
@@ -468,27 +462,13 @@
     def _(j):
         cols = pl.ds(pl.multiple_of(j * chunk, chunk), chunk)
         total = pg_out[:, cols]
+        landed(py_r.at[j], (ny - 1) * dr * chunk * 2 // row_bytes)
         for k in range(1, ny):
-            py_copy(j, k).wait_recv()
             total = total + yr[k - 1, :, cols].astype(F32)
         pg_out[:, cols] = total / STUDENT_TEMP
 
-    def grads():
-        for d in near_z:
-            fn_copy(d).wait_send()
-        for d in late + [0]:
-            for k in range(1, nx):
-                fx_copy(d, k).wait_send()
-        for d in late:
-            fz_copy(d).wait_send()
-
-        @pl.loop(0, nch)
-        def _(j):
-            pc_copy(j).wait_send()
-            for k in range(1, ny):
-                py_copy(j, k).wait_send()
-
-    drain.append(grads)
+    drain.append(lambda: gone(f_s, nx * len(near_z) + (nx - 1) * (len(late) + 1) + len(late)))
+    drain.append(lambda: gone(p_s, (2 * ny - 1) * dr * width * 2 // row_bytes))
     for leave in drain:
         leave()
 
@@ -536,12 +516,10 @@
         pltpu.VMEM((y1, dr, width), BF16),
         pltpu.VMEM((y1, dr, width), BF16),
         dma((2,)),
-        dma((nz,)), dma((nz,)), dma((nz * x1,)), dma((nz * x1,)),
-        dma((nz,)), dma((nz,)), dma((nz * x1,)), dma((nz * x1,)),
-        dma((ITERS, b1)), dma((ITERS, b1)),
-        dma((ITERS + 1, nx * nz - 1)), dma((ITERS + 1, nx * nz - 1)),
-        dma((2,)), dma((2,)), dma((nz * x1,)), dma((nz * x1,)), dma((nz,)), dma((nz,)),
-        dma((nch,)), dma((nch,)), dma((nch, y1)), dma((nch, y1)),
+        dma((nz,)), dma((nz,)), dma((2,)), dma((nz,)),
+        dma((ITERS,)), dma((ITERS + 1,)), dma((2,)), dma((nz,)), dma, dma((nch,)), dma((nch,)),
+        dma, dma, dma, dma, dma, dma,
+        pltpu.VMEM((nx * nz, rows, depth), BF16),
     ]
     return pl.pallas_call(
         functools.partial(kernel, nx, nz, ny),

time: 95.9 us -> 88.4 us (0.922)
  Pallas kernels: 92.7 us -> 85.2 us
    pallas_call x1, Pallas kernels: 92.7 us -> 85.2 us  [shards(): pl.pallas_call(functools.partial(kernel, nx, nz, ny), out_shape=(jax.Shap...]
where the time goes in v3:
time: 88.4 us; the launch traced here: 88.2 us
  Pallas kernels  85.2 us (96%)
  local copies, waits for them, and re-layouts  2.34 us (3%)
    pallas_call x1, Pallas kernels, shards(): pl.pallas_call(functools.partial(kernel, nx, nz, ny), out_shape=(jax.Shap...  85.2 us
    unnamed x4, local copies, waits for them, and re-layouts  2.34 us

profile of v3, /device:TPU:1, one launch (start us, length us, event | category | flops | bytes accessed | tf_op | source)
XLA Modules:
  0.0 88.2 jit_solution(983915175816207963)
XLA Ops:
  0.6 85.2 %shard_map.59 = (f32[32,2048]{1,0:T(8,128)}, f32[64,256]{1,0:T(8,128)}) custom-call(bf16[64,256]{1,0:T(8,128)(2,1)} %sf.1, bf16[64,256]{1,0:T(8,128)(2,1)} %tf.1, bf16[256,2048]{1,0:T(8,128)(2,1)} %sp_hbm.1, bf16[256,2048]{1,0:T(8,128)(2,1)} %tp_hbm.1), custom_call_target="tpu_custom_call" | custom-call | flops 8589934592 | bytes 2097152 | tf_op jit(solution)/shard_map/pallas_call | solution.py:524
  85.9 0.0 copy-start
  85.9 1.7 %copy.8 = f32[32,2048]{1,0:T(8,128)} copy(f32[32,2048]{1,0:T(8,128)} %get-tuple-element.4) | data formatting | bytes 524288
  87.6 0.0 copy-done
  87.6 0.6 copy.9
Async XLA Ops:
  85.9 1.7 %copy-start = (f32[64,256]{1,0:T(8,128)S(1)}, f32[64,256]{1,0:T(8,128)}, u32[]{:S(2)}) copy-start(f32[64,256]{1,0:T(8,128)} %get-tuple-element.5) | copy-start | bytes 196612

commit v4 on v3

--- a/solution.py
+++ b/solution.py
@@ -27,8 +27,8 @@
     nx, nz, ny,
     sf, tf, sp_hbm, tp_hbm,
     pg_out, fg_out,
-    tp, sp, spt, tall, uall, ut, m, e, g,
-    colacc, ps, lse_acc, pay, cinv, ccs,
+    tp, sp, spt, tall, uall, ut, uts, m, e, g,
+    colacc, ps, lse_acc, crop_acc, pay, cinv, ccs, own_col,
     cb, pb,
     ugb, ug0, near, xr, zs, zr,
     pgf, pgb, cr, ys, yr,
@@ -214,17 +214,23 @@
     def compute_e(blk):
         row0 = pl.multiple_of(blk * block, block)
         a = uall[blk]
+        ut[:, pl.ds(row0, block)] = a.T
         acc = jnp.zeros((block, LANES), F32)
+        grad = jnp.zeros((block, depth), F32)
         for j in range(width // tile):
             cols = slice(j * tile, (j + 1) * tile)
             s = jnp.dot(a, sp[:, cols], preferred_element_type=F32)
-            v = jnp.exp2(jnp.minimum(s * (LOG2E / STUDENT_TEMP) - 2.0, 127.0))
-            e[pl.ds(row0, block), cols] = v
+            v = jnp.exp2(jnp.minimum(s * (LOG2E / STUDENT_TEMP), 128.0) - 18.0)
+            half = v.astype(BF16)
+            e[pl.ds(row0, block), cols] = half
             for t in range(tile // LANES):
                 acc += v[:, t * LANES : (t + 1) * LANES]
+            grad += jnp.dot(half, spt[cols, :], preferred_element_type=F32)
+        ugb[0, blk] = grad.astype(BF16)
         for i in range(per):
             col = jnp.sum(acc[i * LANES : (i + 1) * LANES], axis=1, keepdims=True)
             lse_acc[pl.ds(blk * per + i, 1), :] = to_row(col)
+        return grad
 
     def e_blocks(ds):
         @pl.loop(0, len(ds))
@@ -254,9 +260,117 @@
             for t in range(width // LANES):
                 cols = slice(t * LANES, (t + 1) * LANES)
                 acc = acc + m[pl.ds(i * LANES, LANES), cols] * scale[:, cols]
-            ccs[pl.ds(i, 1), :] = to_row(jnp.sum(acc, axis=1, keepdims=True))
+            crop_acc[pl.ds(i, 1), :] = to_row(jnp.sum(acc, axis=1, keepdims=True))
 
         pl.loop(0, groups, unroll=min(4, groups))(body)
+
+    late = far_z[::-1]
+    nch = width // chunk
+
+    def fn_copy(q, d):
+        i = near_z.index(d)
+        return remote(
+            ugb.at[q, (z + d) % nz], near.at[q, i], f_s.at[q], fn_r.at[q, i], to_xz(x, z + d)
+        )
+
+    def fx_copy(q, d, k):
+        xx = (x + k) % nx
+        return remote(
+            ugb.at[q, (z + d) % nz, pl.ds(pl.multiple_of(xx * rows, rows), rows)],
+            xr.at[q, k - 1, d], f_s.at[q], fx_r.at[q, d], to_xz(xx, z),
+        )
+
+    def fz_copy(q, d):
+        return remote(zs.at[q, d], zr.at[q, d], f_s.at[q], fz_r.at[q], to_xz(x, z + d))
+
+    def x_sum(q, d):
+        landed(fx_r.at[q, d], nx - 1)
+        total = ugb[q, (z + d) % nz, pl.ds(my, rows), :].astype(F32) if d else ug0[q, pl.ds(my, rows), :]
+        for k in range(1, nx):
+            total = total + xr[q, k - 1, d].astype(F32)
+        return total
+
+    def z_send(q, d):
+        zs[q, d] = x_sum(q, d).astype(BF16)
+        fz_copy(q, d).start()
+
+    def own_rows(q):
+        total = ug0[q]
+        for i, d in enumerate(near_z):
+            fn_copy(q, d).wait_recv()
+            total = total + near[q, i].astype(F32)
+        ug0[q] = total
+        ugb[q, z] = total.astype(BF16)
+        for k in range(1, nx):
+            fx_copy(q, 0, k).start()
+
+    def f_send(q, d):
+        if d in near_z:
+            fn_copy(q, d).start()
+        elif d:
+            for k in range(1, nx):
+                fx_copy(q, d, k).start()
+
+    def f_total(q):
+        total = x_sum(q, 0)
+        landed(fz_r.at[q], len(late))
+        for d in late:
+            total = total + zr[q, d].astype(F32)
+        return total
+
+    series = near_z + late + [0]
+    pairs = [series[i : i + 2] for i in range(0, nz, 2)]
+
+    def targets(scale):
+        @pl.loop(0, len(pairs))
+        def _(s):
+            blks = [(z + pick(s, [p[i] for p in pairs])) % nz for i in range(2)]
+            scas = [
+                jnp.concatenate([to_col(ccs[pl.ds(blk * per + i, 1), :]) for i in range(per)], axis=0)
+                for blk in blks
+            ]
+            acc = jnp.zeros((2 * block, depth), F32)
+            for j in range(width // tile):
+                cols = slice(j * tile, (j + 1) * tile)
+                both = []
+                for blk, sca in zip(blks, scas):
+                    at = pl.ds(pl.multiple_of(blk * block, block), block)
+                    gh = ((m[at, cols] * sca) * scale[:, cols]).astype(BF16)
+                    g[at, cols] = gh
+                    both.append(gh)
+                acc += jnp.dot(jnp.concatenate(both, axis=0), spt[cols, :], preferred_element_type=F32)
+            for i, blk in enumerate(blks):
+                ugb[1, blk] = acc[i * block : (i + 1) * block].astype(BF16)
+
+            @pl.when(s == len(pairs) - 1)
+            def _():
+                ug0[1] = acc[block:]
+
+            for i, p in enumerate(pairs):
+
+                @pl.when(s == i)
+                def _():
+                    for d in p:
+                        f_send(1, d)
+
+    def scaled_ut(ref):
+        def body(i):
+            cols = pl.ds(pl.multiple_of(i * LANES, LANES), LANES)
+            uts[:, cols] = (ut[:, cols].astype(F32) * ref[pl.ds(i, 1), :]).astype(BF16)
+
+        pl.loop(0, groups, unroll=min(4, groups))(body)
+
+    def probs_part():
+        scaled_ut(cinv)
+
+        @pl.loop(0, nch)
+        def _(j):
+            cols = pl.ds(pl.multiple_of(j * chunk, chunk), chunk)
+            part = jnp.dot(uts[...], e[:, cols], preferred_element_type=F32)
+            for yy in range(ny):
+                for cc in range(2):
+                    d0 = (yy * 2 + cc) * dr
+                    pgf[cc, yy, :, cols] = part[d0 : d0 + dr]
 
     for it in range(ITERS):
         part = colacc[...] if it == 0 else colsum()
@@ -278,10 +392,8 @@
             pay[ITERS] = lse_acc[...].astype(BF16)
             for kx, kz in others:
                 pb_copy(ITERS, kx, kz).start()
-
-            @pl.loop(0, nz)
-            def _(k):
-                ut[:, pl.ds(pl.multiple_of(k * block, block), block)] = uall[k].T
+            for d in u_second:
+                f_send(0, nz - d)
 
         remote(cb.at[it], cb.at[it], cb_s, cb_r.at[it], to_b(bid + 1)).wait_recv()
         total = ps[it]
@@ -291,87 +403,34 @@
         if it == 0:
             u_forward(u_first, 0)
         rowsum(scale)
-        if it == ITERS - 1:
-            cps = scale
-        pay[it] = ccs[...].astype(BF16)
+        pay[it] = crop_acc[...].astype(BF16)
         for kx, kz in others:
             pb_copy(it, kx, kz).start()
         if it == 0:
-            e_blocks([0])
+            landed(ux_r.at[0], nx - 1)
+            ug0[0] = compute_e(z)
         elif it == 1:
+            for d in u_first:
+                f_send(0, nz - d)
             e_blocks(u_second)
         else:
+            targets(scale)
             pb_landed(ITERS)
             cinv[...] = 1.0 / pb_total(ITERS)
+            own_rows(0)
+            for d in late:
+                z_send(0, d)
+            probs_part()
         pb_landed(it)
-        ccs[...] = 1.0 / pb_total(it)
+        if it < ITERS - 1:
+            ccs[...] = 1.0 / pb_total(it)
+        else:
+            ccs[...] = 1.0 / (pb_total(it) * ccs[...])
 
 
     drain.append(lambda: gone(u_s, (nx - 1) * nz + nz - 1))
     drain.append(lambda: remote(cb, cb, cb_s, cb_r.at[0], to_b(bid + 1)).wait_send())
     drain.append(lambda: remote(pb, pb, pb_s, pb_r.at[0], to_xz(x, z + 1)).wait_send())
-
-    def fn_copy(d):
-        i = near_z.index(d)
-        return remote(
-            ugb.at[(z + d) % nz], near.at[i], f_s, fn_r.at[i], to_xz(x, z + d)
-        )
-
-    def fx_copy(d, k):
-        xx = (x + k) % nx
-        return remote(
-            ugb.at[(z + d) % nz, pl.ds(pl.multiple_of(xx * rows, rows), rows)],
-            xr.at[k - 1, d], f_s, fx_r.at[d], to_xz(xx, z),
-        )
-
-    def fz_copy(d):
-        return remote(zs.at[d], zr.at[d], f_s, fz_r, to_xz(x, z + d))
-
-    late = far_z[::-1]
-    series = near_z + late + [0]
-    pairs = [series[i : i + 2] for i in range(0, nz, 2)]
-
-    @pl.loop(0, len(pairs))
-    def _(s):
-        blks = [(z + pick(s, [p[i] for p in pairs])) % nz for i in range(2)]
-        invs, scas = [
-            [
-                jnp.concatenate([to_col(ref[pl.ds(blk * per + i, 1), :]) for i in range(per)], axis=0)
-                for blk in blks
-            ]
-            for ref in (cinv, ccs)
-        ]
-        acc = jnp.zeros((2 * block, depth), F32)
-        for j in range(width // tile):
-            cols = slice(j * tile, (j + 1) * tile)
-            both = []
-            for blk, inv, sca in zip(blks, invs, scas):
-                at = pl.ds(pl.multiple_of(blk * block, block), block)
-                prob = e[at, cols] * inv
-                target = (m[at, cols] * sca) * cps[:, cols]
-                gh = (prob - target).astype(BF16)
-                g[at, cols] = gh
-                both.append(gh)
-            acc += jnp.dot(jnp.concatenate(both, axis=0), spt[cols, :], preferred_element_type=F32)
-        for i, blk in enumerate(blks):
-            ugb[blk] = acc[i * block : (i + 1) * block].astype(BF16)
-
-        @pl.when(s == len(pairs) - 1)
-        def _():
-            ug0[...] = acc[block:]
-
-        for i, p in enumerate(pairs):
-
-            @pl.when(s == i)
-            def _():
-                for d in p:
-                    if d in near_z:
-                        fn_copy(d).start()
-                    elif d:
-                        for k in range(1, nx):
-                            fx_copy(d, k).start()
-
-    nch = width // chunk
 
     def pc_copy(j):
         cols = pl.ds(pl.multiple_of(j * chunk, chunk), chunk)
@@ -395,44 +454,26 @@
             py_copy(j, k).start()
         pg_out[:, cols] = pgf[c, y, :, cols] + cr[y, :, cols].astype(F32)
 
-    def x_sum(d):
-        landed(fx_r.at[d], nx - 1)
-        total = ugb[(z + d) % nz, pl.ds(my, rows), :].astype(F32) if d else ug0[pl.ds(my, rows), :]
-        for k in range(1, nx):
-            total = total + xr[k - 1, d].astype(F32)
-        return total
-
-    def z_send(d):
-        zs[d] = x_sum(d).astype(BF16)
-        fz_copy(d).start()
-
-    def own_rows():
-        total = ug0[...]
-        for i, d in enumerate(near_z):
-            fn_copy(d).wait_recv()
-            total = total + near[i].astype(F32)
-        ug0[...] = total
-        ugb[z] = total.astype(BF16)
-        for k in range(1, nx):
-            fx_copy(0, k).start()
-
-    after = {1: ["own"], 2: late[:2], 3: late[2:3]}
+    scaled_ut(ccs)
+
+    after = {0: ["own"] + late[:1], 1: late[1:2], 2: late[2:4]}
     after = {j: a for j, a in after.items() if j < nch}
     done = [d for a in after.values() for d in a]
     rest = (["own"] if "own" not in done else []) + [d for d in late if d not in done]
 
     def act(d):
-        own_rows() if d == "own" else z_send(d)
+        own_rows(1) if d == "own" else z_send(1, d)
 
     @pl.loop(0, nch)
     def _(j):
         cols = pl.ds(pl.multiple_of(j * chunk, chunk), chunk)
-        part = jnp.dot(ut[...], g[:, cols], preferred_element_type=F32)
+        part = jnp.dot(uts[...], g[:, cols], preferred_element_type=F32)
         for yy in range(ny):
             for cc in range(2):
                 d0 = (yy * 2 + cc) * dr
-                pgf[cc, yy, :, cols] = part[d0 : d0 + dr]
-                pgb[cc, yy, :, cols] = part[d0 : d0 + dr].astype(BF16)
+                diff = pgf[cc, yy, :, cols] - part[d0 : d0 + dr]
+                pgf[cc, yy, :, cols] = diff
+                pgb[cc, yy, :, cols] = diff.astype(BF16)
         pc_copy(j).start()
 
         @pl.when(j > 0)
@@ -449,10 +490,12 @@
     pc_sum(nch - 1)
     for d in rest:
         act(d)
-    total = x_sum(0)
-    landed(fz_r, len(late))
-    for d in late:
-        total = total + zr[d].astype(F32)
+    part = z * per + my // LANES
+    for q, ref in enumerate((cinv, ccs)):
+        own_col[q] = jnp.broadcast_to(to_col(ref[pl.ds(part, 1), :]), (LANES, LANES))
+    low = pl.multiple_of(my % LANES, min(rows, LANES))
+    inv, rho = [own_col[q, pl.ds(low, rows), 0:1] for q in range(2)]
+    total = f_total(0) * inv - f_total(1) * rho
     total = total / STUDENT_TEMP
     unit, norm = unit_rows(sf[...])
     inner = jnp.sum(unit * total, axis=1, keepdims=True)
@@ -467,7 +510,8 @@
             total = total + yr[k - 1, :, cols].astype(F32)
         pg_out[:, cols] = total / STUDENT_TEMP
 
-    drain.append(lambda: gone(f_s, nx * len(near_z) + (nx - 1) * (len(late) + 1) + len(late)))
+    drain.append(lambda: gone(f_s.at[0], nx * len(near_z) + (nx - 1) * (len(late) + 1) + len(late)))
+    drain.append(lambda: gone(f_s.at[1], nx * len(near_z) + (nx - 1) * (len(late) + 1) + len(late)))
     drain.append(lambda: gone(p_s, (2 * ny - 1) * dr * width * 2 // row_bytes))
     for leave in drain:
         leave()
@@ -493,23 +537,26 @@
         pltpu.VMEM((nz, block, depth), BF16),
         pltpu.VMEM((nz, block, depth), BF16),
         pltpu.VMEM((depth, crops), BF16),
+        pltpu.VMEM((depth, crops), BF16),
         pltpu.VMEM((crops, width), F32),
-        pltpu.VMEM((crops, width), F32),
+        pltpu.VMEM((crops, width), BF16),
         pltpu.VMEM((crops, width), BF16),
         pltpu.VMEM((8, width), F32),
         pltpu.VMEM((ITERS, 1, width), F32),
         pltpu.VMEM((groups, LANES), F32),
+        pltpu.VMEM((groups, LANES), F32),
         pltpu.VMEM((ITERS + 1, groups, LANES), BF16),
         pltpu.VMEM((groups, LANES), F32),
         pltpu.VMEM((groups, LANES), F32),
+        pltpu.VMEM((2, LANES, LANES), F32),
         pltpu.VMEM((ITERS, b1, 1, width), F32),
         pltpu.VMEM((ITERS + 1, nx * nz - 1, groups, LANES), BF16),
-        pltpu.VMEM((nz, block, depth), BF16),
-        pltpu.VMEM((block, depth), F32),
-        pltpu.VMEM((2, block, depth), BF16),
-        pltpu.VMEM((x1, nz, rows, depth), BF16),
-        pltpu.VMEM((nz, rows, depth), BF16),
-        pltpu.VMEM((nz, rows, depth), BF16),
+        pltpu.VMEM((2, nz, block, depth), BF16),
+        pltpu.VMEM((2, block, depth), F32),
+        pltpu.VMEM((2, 2, block, depth), BF16),
+        pltpu.VMEM((2, x1, nz, rows, depth), BF16),
+        pltpu.VMEM((2, nz, rows, depth), BF16),
+        pltpu.VMEM((2, nz, rows, depth), BF16),
         pltpu.VMEM((2, ny, dr, width), F32),
         pltpu.VMEM((2, ny, dr, width), BF16),
         pltpu.VMEM((ny, dr, width), BF16),
@@ -517,8 +564,8 @@
         pltpu.VMEM((y1, dr, width), BF16),
         dma((2,)),
         dma((nz,)), dma((nz,)), dma((2,)), dma((nz,)),
-        dma((ITERS,)), dma((ITERS + 1,)), dma((2,)), dma((nz,)), dma, dma((nch,)), dma((nch,)),
-        dma, dma, dma, dma, dma, dma,
+        dma((ITERS,)), dma((ITERS + 1,)), dma((2, 2)), dma((2, nz)), dma((2,)), dma((nch,)), dma((nch,)),
+        dma, dma, dma, dma, dma((2,)), dma,
         pltpu.VMEM((nx * nz, rows, depth), BF16),
     ]
     return pl.pallas_call(
@@ -534,7 +581,7 @@
             collective_id=0, has_side_effects=True, vmem_limit_bytes=60 * 1024 * 1024
         ),
         cost_estimate=pl.CostEstimate(
-            flops=8 * crops * width * depth, bytes_accessed=4 * depth * width,
+            flops=12 * crops * width * depth, bytes_accessed=4 * depth * width,
             transcendentals=2 * crops * width,
         ),
     )(student_feats, teacher_feats, student_protos, teacher_protos)

time: 88.4 us -> 82.5 us (0.933)
  Pallas kernels: 85.2 us -> 79.4 us
    pallas_call x1, Pallas kernels: 85.2 us -> 79.4 us  [shards(): pl.pallas_call(functools.partial(kernel, nx, nz, ny), out_shape=(jax.Shap...]
where the time goes in v4:
time: 82.5 us; the launch traced here: 82.4 us
  Pallas kernels  79.4 us (96%)
  local copies, waits for them, and re-layouts  2.34 us (3%)
    pallas_call x1, Pallas kernels, shards(): pl.pallas_call(functools.partial(kernel, nx, nz, ny), out_shape=(jax.Shap...  79.4 us
    unnamed x4, local copies, waits for them, and re-layouts  2.34 us

profile of v4, /device:TPU:1, one launch (start us, length us, event | category | flops | bytes accessed | tf_op | source)
XLA Modules:
  0.0 82.4 jit_solution(1700079962236912300)
XLA Ops:
  0.6 79.4 %shard_map.59 = (f32[32,2048]{1,0:T(8,128)}, f32[64,256]{1,0:T(8,128)}) custom-call(bf16[64,256]{1,0:T(8,128)(2,1)} %sf.1, bf16[64,256]{1,0:T(8,128)(2,1)} %tf.1, bf16[256,2048]{1,0:T(8,128)(2,1)} %sp_hbm.1, bf16[256,2048]{1,0:T(8,128)(2,1)} %tp_hbm.1), custom_call_target="tpu_custom_call" | custom-call | flops 12884901888 | bytes 2097152 | tf_op jit(solution)/shard_map/pallas_call | solution.py:571
  80.0 0.0 copy-start
  80.0 1.7 %copy.8 = f32[32,2048]{1,0:T(8,128)} copy(f32[32,2048]{1,0:T(8,128)} %get-tuple-element.4) | data formatting | bytes 524288
  81.7 0.0 copy-done
  81.7 0.6 copy.9
Async XLA Ops:
  80.0 1.7 %copy-start = (f32[64,256]{1,0:T(8,128)S(1)}, f32[64,256]{1,0:T(8,128)}, u32[]{:S(2)}) copy-start(f32[64,256]{1,0:T(8,128)} %get-tuple-element.5) | copy-start | bytes 196612

commit v5 on v4

--- a/solution.py
+++ b/solution.py
@@ -28,12 +28,12 @@
     sf, tf, sp_hbm, tp_hbm,
     pg_out, fg_out,
     tp, sp, spt, tall, uall, ut, uts, m, e, g,
-    colacc, ps, lse_acc, crop_acc, pay, cinv, ccs, own_col,
-    cb, pb,
+    colacc, racc, ps, lse_acc, crop_acc, pay, pay_l, cinv, ccs, own_col,
+    cb, pb, pbl,
     ugb, ug0, near, xr, zs, zr,
     pgf, pgb, cr, ys, yr,
     local_s,
-    tz_r, tx_r, uz_r, ux_r, cb_r, pb_r, fn_r, fx_r, fz_r, pc_r, py_r,
+    tz_r, tx_r, uz_r, ux_r, cb_r, pb_r, pbl_r, fn_r, fx_r, fz_r, pc_r, py_r,
     t_s, u_s, cb_s, pb_s, f_s, p_s,
     spare,
 ):
@@ -189,26 +189,35 @@
 
     drain.append(lambda: gone(t_s, (nx - 1) * (1 + len(far_z)) + len(far_z) + nx * len(near_z)))
 
-    def cb_copy(it, k):
+    def cb_copy(it, h, k):
         return remote(
-            ps.at[it], cb.at[it, k - 1], cb_s, cb_r.at[it], to_b(bid + k)
+            ps.at[it, h], cb.at[it, h, k - 1], cb_s, cb_r.at[it, h], to_b(bid + k)
         )
 
-    def pb_copy(it, kx, kz):
+    def pb_copy(it, h, kx, kz):
         i = kx * nz + kz - 1
         return remote(
-            pay.at[it], pb.at[it, i], pb_s, pb_r.at[it], to_xz(x + kx, z + kz)
+            pay.at[it, h], pb.at[it, h, i], pb_s, pb_r.at[it, h], to_xz(x + kx, z + kz)
         )
 
+    def pbl_copy(kx, kz):
+        i = kx * nz + kz - 1
+        return remote(pay_l, pbl.at[i], pb_s, pbl_r, to_xz(x + kx, z + kz))
+
     others = [(kx, kz) for kx in range(nx) for kz in range(nz) if kx or kz]
 
-    def pb_landed(it):
-        remote(pb.at[it], pb.at[it], pb_s, pb_r.at[it], to_xz(x, z + 1)).wait_recv()
-
-    def pb_total(it):
-        total = pay[it].astype(F32)
+    def pb_total(it, h):
+        remote(pb.at[it, h], pb.at[it, h], pb_s, pb_r.at[it, h], to_xz(x, z + 1)).wait_recv()
+        total = pay[it, h].astype(F32)
         for i in range(nx * nz - 1):
-            total = total + pb[it, i].astype(F32)
+            total = total + pb[it, h, i].astype(F32)
+        return total
+
+    def pbl_total():
+        remote(pbl, pbl, pb_s, pbl_r, to_xz(x, z + 1)).wait_recv()
+        total = pay_l[...].astype(F32)
+        for i in range(nx * nz - 1):
+            total = total + pbl[i].astype(F32)
         return total
 
     def compute_e(blk):
@@ -245,24 +254,50 @@
             for k in range(1, nx):
                 ux(d, k).start()
 
-    def colsum():
-        def body(i, acc):
-            col = to_col(ccs[pl.ds(i, 1), :])
+    hw, hg = width // 2, groups // 2
+
+    def crop_col(i, keep):
+        at = pl.ds(pl.multiple_of(i * LANES, LANES), LANES)
+        if keep is None:
+            return racc[at, :]
+        col = jnp.broadcast_to(to_col(ccs[pl.ds(i, 1), :]), (LANES, LANES))
+        if keep:
+            racc[at, :] = col
+        return col
+
+    def colsum(h, lo, n, keep):
+        def body(j, acc):
+            i = h * hg + j
+            col = crop_col(i, keep)
             for q in range(LANES // 8):
-                acc = acc + m[pl.ds(i * LANES + q * 8, 8), :] * col[q * 8 : (q + 1) * 8]
+                part = m[pl.ds(pl.multiple_of(i * LANES + q * 8, 8), 8), lo : lo + n]
+                acc = acc + part * col[q * 8 : (q + 1) * 8, 0:1]
             return acc
 
-        return lax.fori_loop(0, groups, body, jnp.zeros((8, width), F32), unroll=min(4, groups))
-
-    def rowsum(scale):
+        return lax.fori_loop(0, hg, body, jnp.zeros((8, n), F32), unroll=min(4, hg))
+
+    def rowsum_first(scale):
         def body(i):
+            at = pl.ds(pl.multiple_of(i * LANES, LANES), LANES)
             acc = jnp.zeros((LANES, LANES), F32)
-            for t in range(width // LANES):
+            for t in range(hw // LANES):
                 cols = slice(t * LANES, (t + 1) * LANES)
-                acc = acc + m[pl.ds(i * LANES, LANES), cols] * scale[:, cols]
+                acc = acc + m[at, cols] * scale[:, cols]
+            racc[at, :] = acc
+
+        pl.loop(0, groups, unroll=min(2, groups))(body)
+
+    def rowsum_second(scale, h):
+        def body(j):
+            i = h * hg + j
+            at = pl.ds(pl.multiple_of(i * LANES, LANES), LANES)
+            acc = racc[at, :]
+            for t in range(hw // LANES):
+                cols = slice(t * LANES, (t + 1) * LANES)
+                acc = acc + m[at, hw + t * LANES : hw + (t + 1) * LANES] * scale[:, cols]
             crop_acc[pl.ds(i, 1), :] = to_row(jnp.sum(acc, axis=1, keepdims=True))
 
-        pl.loop(0, groups, unroll=min(4, groups))(body)
+        pl.loop(0, hg, unroll=min(4, hg))(body)
 
     late = far_z[::-1]
     nch = width // chunk
@@ -372,11 +407,31 @@
                     d0 = (yy * 2 + cc) * dr
                     pgf[cc, yy, :, cols] = part[d0 : d0 + dr]
 
+    def send_ps(it, h, part):
+        ps[it, h] = jnp.sum(part, axis=0, keepdims=True)
+        for k in range(1, nb):
+            cb_copy(it, h, k).start()
+
+    def proto_scale(it, h):
+        remote(cb.at[it, h], cb.at[it, h], cb_s, cb_r.at[it, h], to_b(bid + 1)).wait_recv()
+        total = ps[it, h]
+        for k in range(1, nb):
+            total = total + cb[it, h, k - 1]
+        return 1.0 / total
+
+    def crop_half(h):
+        return pl.ds(h * hg, hg)
+
     for it in range(ITERS):
-        part = colacc[...] if it == 0 else colsum()
-        ps[it] = jnp.sum(part, axis=0, keepdims=True)
-        for k in range(1, nb):
-            cb_copy(it, k).start()
+        if it == 0:
+            for h in range(2):
+                send_ps(it, h, colacc[:, h * hw : (h + 1) * hw])
+        else:
+            ccs[crop_half(0), :] = 1.0 / pb_total(it - 1, 0)
+            colacc[...] = colsum(0, 0, width, False)
+            ccs[crop_half(1), :] = 1.0 / pb_total(it - 1, 1)
+            for h in range(2):
+                send_ps(it, h, colacc[:, h * hw : (h + 1) * hw] + colsum(1, h * hw, hw, None if h else True))
         if it == 0:
             load_sp.wait()
 
@@ -389,23 +444,21 @@
             u_forward(u_second, 1)
             e_blocks(u_first)
         else:
-            pay[ITERS] = lse_acc[...].astype(BF16)
+            pay_l[...] = lse_acc[...].astype(BF16)
             for kx, kz in others:
-                pb_copy(ITERS, kx, kz).start()
+                pbl_copy(kx, kz).start()
             for d in u_second:
                 f_send(0, nz - d)
-
-        remote(cb.at[it], cb.at[it], cb_s, cb_r.at[it], to_b(bid + 1)).wait_recv()
-        total = ps[it]
-        for k in range(1, nb):
-            total = total + cb[it, k - 1]
-        scale = 1.0 / total
+        scales = [proto_scale(it, 0)]
         if it == 0:
             u_forward(u_first, 0)
-        rowsum(scale)
-        pay[it] = crop_acc[...].astype(BF16)
-        for kx, kz in others:
-            pb_copy(it, kx, kz).start()
+        rowsum_first(scales[0])
+        scales.append(proto_scale(it, 1))
+        for h in range(2):
+            rowsum_second(scales[1], h)
+            pay[it, h] = crop_acc[crop_half(h), :].astype(BF16)
+            for kx, kz in others:
+                pb_copy(it, h, kx, kz).start()
         if it == 0:
             landed(ux_r.at[0], nx - 1)
             ug0[0] = compute_e(z)
@@ -414,23 +467,19 @@
                 f_send(0, nz - d)
             e_blocks(u_second)
         else:
-            targets(scale)
-            pb_landed(ITERS)
-            cinv[...] = 1.0 / pb_total(ITERS)
+            targets(jnp.concatenate(scales, axis=1))
+            cinv[...] = 1.0 / pbl_total()
             own_rows(0)
             for d in late:
                 z_send(0, d)
             probs_part()
-        pb_landed(it)
-        if it < ITERS - 1:
-            ccs[...] = 1.0 / pb_total(it)
-        else:
-            ccs[...] = 1.0 / (pb_total(it) * ccs[...])
-
+    for h in range(2):
+        ccs[crop_half(h), :] = 1.0 / (pb_total(ITERS - 1, h) * ccs[crop_half(h), :])
 
     drain.append(lambda: gone(u_s, (nx - 1) * nz + nz - 1))
-    drain.append(lambda: remote(cb, cb, cb_s, cb_r.at[0], to_b(bid + 1)).wait_send())
-    drain.append(lambda: remote(pb, pb, pb_s, pb_r.at[0], to_xz(x, z + 1)).wait_send())
+    drain.append(lambda: remote(cb, cb, cb_s, cb_r.at[0, 0], to_b(bid + 1)).wait_send())
+    drain.append(lambda: remote(pb, pb, pb_s, pb_r.at[0, 0], to_xz(x, z + 1)).wait_send())
+    drain.append(lambda: remote(pbl, pbl, pb_s, pbl_r, to_xz(x, z + 1)).wait_send())
 
     def pc_copy(j):
         cols = pl.ds(pl.multiple_of(j * chunk, chunk), chunk)
@@ -496,7 +545,6 @@
     low = pl.multiple_of(my % LANES, min(rows, LANES))
     inv, rho = [own_col[q, pl.ds(low, rows), 0:1] for q in range(2)]
     total = f_total(0) * inv - f_total(1) * rho
-    total = total / STUDENT_TEMP
     unit, norm = unit_rows(sf[...])
     inner = jnp.sum(unit * total, axis=1, keepdims=True)
     fg_out[...] = (total - unit * inner) / norm
@@ -508,13 +556,18 @@
         landed(py_r.at[j], (ny - 1) * dr * chunk * 2 // row_bytes)
         for k in range(1, ny):
             total = total + yr[k - 1, :, cols].astype(F32)
-        pg_out[:, cols] = total / STUDENT_TEMP
+        pg_out[:, cols] = total
 
     drain.append(lambda: gone(f_s.at[0], nx * len(near_z) + (nx - 1) * (len(late) + 1) + len(late)))
     drain.append(lambda: gone(f_s.at[1], nx * len(near_z) + (nx - 1) * (len(late) + 1) + len(late)))
     drain.append(lambda: gone(p_s, (2 * ny - 1) * dr * width * 2 // row_bytes))
     for leave in drain:
         leave()
+
+
+def scale_out(a, b, a_out, b_out):
+    a_out[...] = a[...] / STUDENT_TEMP
+    b_out[...] = b[...] / STUDENT_TEMP
 
 
 def shards(nx, nz, ny, student_feats, teacher_feats, student_protos, teacher_protos):
@@ -542,15 +595,18 @@
         pltpu.VMEM((crops, width), BF16),
         pltpu.VMEM((crops, width), BF16),
         pltpu.VMEM((8, width), F32),
-        pltpu.VMEM((ITERS, 1, width), F32),
+        pltpu.VMEM((crops, LANES), F32),
+        pltpu.VMEM((ITERS, 2, 1, width // 2), F32),
         pltpu.VMEM((groups, LANES), F32),
         pltpu.VMEM((groups, LANES), F32),
-        pltpu.VMEM((ITERS + 1, groups, LANES), BF16),
+        pltpu.VMEM((ITERS, 2, groups // 2, LANES), BF16),
+        pltpu.VMEM((groups, LANES), BF16),
         pltpu.VMEM((groups, LANES), F32),
         pltpu.VMEM((groups, LANES), F32),
         pltpu.VMEM((2, LANES, LANES), F32),
-        pltpu.VMEM((ITERS, b1, 1, width), F32),
-        pltpu.VMEM((ITERS + 1, nx * nz - 1, groups, LANES), BF16),
+        pltpu.VMEM((ITERS, 2, b1, 1, width // 2), F32),
+        pltpu.VMEM((ITERS, 2, nx * nz - 1, groups // 2, LANES), BF16),
+        pltpu.VMEM((nx * nz - 1, groups, LANES), BF16),
         pltpu.VMEM((2, nz, block, depth), BF16),
         pltpu.VMEM((2, block, depth), F32),
         pltpu.VMEM((2, 2, block, depth), BF16),
@@ -564,11 +620,11 @@
         pltpu.VMEM((y1, dr, width), BF16),
         dma((2,)),
         dma((nz,)), dma((nz,)), dma((2,)), dma((nz,)),
-        dma((ITERS,)), dma((ITERS + 1,)), dma((2, 2)), dma((2, nz)), dma((2,)), dma((nch,)), dma((nch,)),
+        dma((ITERS, 2)), dma((ITERS, 2)), dma, dma((2, 2)), dma((2, nz)), dma((2,)), dma((nch,)), dma((nch,)),
         dma, dma, dma, dma, dma((2,)), dma,
         pltpu.VMEM((nx * nz, rows, depth), BF16),
     ]
-    return pl.pallas_call(
+    outs = pl.pallas_call(
         functools.partial(kernel, nx, nz, ny),
         out_shape=(
             jax.ShapeDtypeStruct((dr, width), F32),
@@ -585,6 +641,12 @@
             transcendentals=2 * crops * width,
         ),
     )(student_feats, teacher_feats, student_protos, teacher_protos)
+    return pl.pallas_call(
+        scale_out,
+        out_shape=tuple(jax.ShapeDtypeStruct(o.shape, o.dtype) for o in outs),
+        in_specs=[vmem, vmem],
+        out_specs=(vmem, vmem),
+    )(*outs)
 
 
 def solution(mesh, nz=8):

time: 82.5 us -> 79.8 us (0.967)
  local copies, waits for them, and re-layouts: 2.34 us -> 0 us
    unnamed x4 -> x0, local copies, waits for them, and re-layouts: 2.34 us -> none
    pallas_call x1, Pallas kernels: 79.4 us -> 77.3 us  [shards(): pl.pallas_call(functools.partial(kernel, nx, nz, ny), out_shape=(jax.Shap...]
    pallas_call x0 -> x1, Pallas kernels: none -> 1.69 us  [shards(): pl.pallas_call(scale_out, out_shape=tuple((jax.ShapeDtypeStruct(o.shape,...]
where the time goes in v5:
time: 79.8 us; the launch traced here: 79.7 us
  Pallas kernels  79 us (99%)
    pallas_call x1, Pallas kernels, shards(): pl.pallas_call(functools.partial(kernel, nx, nz, ny), out_shape=(jax.Shap...  77.3 us
    pallas_call x1, Pallas kernels, shards(): pl.pallas_call(scale_out, out_shape=tuple((jax.ShapeDtypeStruct(o.shape,...  1.69 us

profile of v5, /device:TPU:1, one launch (start us, length us, event | category | flops | bytes accessed | tf_op | source)
XLA Modules:
  0.0 79.7 jit_solution(4727247195510055844)
XLA Ops:
  0.6 77.3 %shard_map.59 = (f32[32,2048]{1,0:T(8,128)}, f32[64,256]{1,0:T(8,128)}) custom-call(bf16[64,256]{1,0:T(8,128)(2,1)} %sf.1, bf16[64,256]{1,0:T(8,128)(2,1)} %tf.1, bf16[256,2048]{1,0:T(8,128)(2,1)} %sp_hbm.1, bf16[256,2048]{1,0:T(8,128)(2,1)} %tp_hbm.1), custom_call_target="tpu_custom_call" | custom-call | flops 12884901888 | bytes 2097152 | tf_op jit(solution)/shard_map/pallas_call | solution.py:627
  78.0 1.7 %shard_map.60 = (f32[32,2048]{1,0:T(8,128)}, f32[64,256]{1,0:T(8,128)}) custom-call(f32[32,2048]{1,0:T(8,128)} %get-tuple-element.4.a, f32[64,256]{1,0:T(8,128)} %get-tuple-element.5.b), custom_call_target="tpu_custom_call" | custom-call | tf_op jit(solution)/shard_map/pallas_call | solution.py:644

commit v6 on v5

--- a/solution.py
+++ b/solution.py
@@ -205,6 +205,7 @@
         return remote(pay_l, pbl.at[i], pb_s, pbl_r, to_xz(x + kx, z + kz))
 
     others = [(kx, kz) for kx in range(nx) for kz in range(nz) if kx or kz]
+    others.sort(key=lambda p: -min(p[0], nx - p[0]) - min(p[1], nz - p[1]))
 
     def pb_total(it, h):
         remote(pb.at[it, h], pb.at[it, h], pb_s, pb_r.at[it, h], to_xz(x, z + 1)).wait_recv()
@@ -270,11 +271,15 @@
             i = h * hg + j
             col = crop_col(i, keep)
             for q in range(LANES // 8):
-                part = m[pl.ds(pl.multiple_of(i * LANES + q * 8, 8), 8), lo : lo + n]
-                acc = acc + part * col[q * 8 : (q + 1) * 8, 0:1]
+                at = pl.ds(pl.multiple_of(i * LANES + q * 8, 8), 8)
+                w = col[q * 8 : (q + 1) * 8]
+                acc = tuple(
+                    a + m[at, lo + t * LANES : lo + (t + 1) * LANES] * w for t, a in enumerate(acc)
+                )
             return acc
 
-        return lax.fori_loop(0, hg, body, jnp.zeros((8, n), F32), unroll=min(4, hg))
+        init = tuple(jnp.zeros((8, LANES), F32) for _ in range(n // LANES))
+        return jnp.concatenate(lax.fori_loop(0, hg, body, init, unroll=min(4, hg)), axis=1)
 
     def rowsum_first(scale):
         def body(i):
@@ -444,9 +449,6 @@
             u_forward(u_second, 1)
             e_blocks(u_first)
         else:
-            pay_l[...] = lse_acc[...].astype(BF16)
-            for kx, kz in others:
-                pbl_copy(kx, kz).start()
             for d in u_second:
                 f_send(0, nz - d)
         scales = [proto_scale(it, 0)]
@@ -466,6 +468,9 @@
             for d in u_first:
                 f_send(0, nz - d)
             e_blocks(u_second)
+            pay_l[...] = lse_acc[...].astype(BF16)
+            for kx, kz in others:
+                pbl_copy(kx, kz).start()
         else:
             targets(jnp.concatenate(scales, axis=1))
             cinv[...] = 1.0 / pbl_total()

time: 79.8 us -> 79.2 us (level)
  no operation moved by 1% of the time
where the time goes in v6:
time: 79.2 us; the launch traced here: 79.1 us
  Pallas kernels  78.4 us (99%)
    pallas_call x1, Pallas kernels, shards(): pl.pallas_call(functools.partial(kernel, nx, nz, ny), out_shape=(jax.Shap...  76.8 us
    pallas_call x1, Pallas kernels, shards(): pl.pallas_call(scale_out, out_shape=tuple((jax.ShapeDtypeStruct(o.shape,...  1.69 us

profile of v6, /device:TPU:1, one launch (start us, length us, event | category | flops | bytes accessed | tf_op | source)
XLA Modules:
  0.0 79.1 jit_solution(16733803954314617610)
XLA Ops:
  0.6 76.8 %shard_map.59 = (f32[32,2048]{1,0:T(8,128)}, f32[64,256]{1,0:T(8,128)}) custom-call(bf16[64,256]{1,0:T(8,128)(2,1)} %sf.1, bf16[64,256]{1,0:T(8,128)(2,1)} %tf.1, bf16[256,2048]{1,0:T(8,128)(2,1)} %sp_hbm.1, bf16[256,2048]{1,0:T(8,128)(2,1)} %tp_hbm.1), custom_call_target="tpu_custom_call" | custom-call | flops 12884901888 | bytes 2097152 | tf_op jit(solution)/shard_map/pallas_call | solution.py:632
  77.4 1.7 %shard_map.60 = (f32[32,2048]{1,0:T(8,128)}, f32[64,256]{1,0:T(8,128)}) custom-call(f32[32,2048]{1,0:T(8,128)} %get-tuple-element.4.a, f32[64,256]{1,0:T(8,128)} %get-tuple-element.5.b), custom_call_target="tpu_custom_call" | custom-call | tf_op jit(solution)/shard_map/pallas_call | solution.py:649

commit v7 on v6

--- a/solution.py
+++ b/solution.py
@@ -154,8 +154,9 @@
     for d in near_z:
         trow(d).start()
     load_tp.wait()
-    compute_m(z)
-    for d in far_z:
+    for i, d in enumerate(far_z):
+        if i == min(2, len(far_z) - 1):
+            compute_m(z)
         tz(d).wait_recv()
         for k in range(1, nx):
             tx(d, k).start()
@@ -230,7 +231,7 @@
         for j in range(width // tile):
             cols = slice(j * tile, (j + 1) * tile)
             s = jnp.dot(a, sp[:, cols], preferred_element_type=F32)
-            v = jnp.exp2(jnp.minimum(s * (LOG2E / STUDENT_TEMP), 128.0) - 18.0)
+            v = jnp.exp2(jnp.minimum(s * (LOG2E / STUDENT_TEMP), 128.0) - 2.0)
             half = v.astype(BF16)
             e[pl.ds(row0, block), cols] = half
             for t in range(tile // LANES):
@@ -393,15 +394,15 @@
                     for d in p:
                         f_send(1, d)
 
-    def scaled_ut(ref):
+    def scaled_ut(ref, factor=1.0):
         def body(i):
             cols = pl.ds(pl.multiple_of(i * LANES, LANES), LANES)
-            uts[:, cols] = (ut[:, cols].astype(F32) * ref[pl.ds(i, 1), :]).astype(BF16)
+            uts[:, cols] = (ut[:, cols].astype(F32) * (ref[pl.ds(i, 1), :] * factor)).astype(BF16)
 
         pl.loop(0, groups, unroll=min(4, groups))(body)
 
     def probs_part():
-        scaled_ut(cinv)
+        scaled_ut(cinv, 4096.0)
 
         @pl.loop(0, nch)
         def _(j):
@@ -410,7 +411,7 @@
             for yy in range(ny):
                 for cc in range(2):
                     d0 = (yy * 2 + cc) * dr
-                    pgf[cc, yy, :, cols] = part[d0 : d0 + dr]
+                    pgf[cc, yy, :, cols] = part[d0 : d0 + dr] * (1.0 / 4096.0)
 
     def send_ps(it, h, part):
         ps[it, h] = jnp.sum(part, axis=0, keepdims=True)
@@ -549,7 +550,7 @@
         own_col[q] = jnp.broadcast_to(to_col(ref[pl.ds(part, 1), :]), (LANES, LANES))
     low = pl.multiple_of(my % LANES, min(rows, LANES))
     inv, rho = [own_col[q, pl.ds(low, rows), 0:1] for q in range(2)]
-    total = f_total(0) * inv - f_total(1) * rho
+    total = jnp.where(inv > 0.0, f_total(0) * inv, 0.0) - f_total(1) * rho
     unit, norm = unit_rows(sf[...])
     inner = jnp.sum(unit * total, axis=1, keepdims=True)
     fg_out[...] = (total - unit * inner) / norm

time: 79.2 us -> 79.2 us (level)
  no operation moved by 1% of the time
where the time goes in v7:
time: 79.2 us; the launch traced here: 79.1 us
  Pallas kernels  78.4 us (99%)
    pallas_call x1, Pallas kernels, shards(): pl.pallas_call(functools.partial(kernel, nx, nz, ny), out_shape=(jax.Shap...  76.8 us
    pallas_call x1, Pallas kernels, shards(): pl.pallas_call(scale_out, out_shape=tuple((jax.ShapeDtypeStruct(o.shape,...  1.69 us

profile of v7, /device:TPU:1, one launch (start us, length us, event | category | flops | bytes accessed | tf_op | source)
XLA Modules:
  0.0 79.1 jit_solution(17176764686905610723)
XLA Ops:
  0.6 76.8 %shard_map.59 = (f32[32,2048]{1,0:T(8,128)}, f32[64,256]{1,0:T(8,128)}) custom-call(bf16[64,256]{1,0:T(8,128)(2,1)} %sf.1, bf16[64,256]{1,0:T(8,128)(2,1)} %tf.1, bf16[256,2048]{1,0:T(8,128)(2,1)} %sp_hbm.1, bf16[256,2048]{1,0:T(8,128)(2,1)} %tp_hbm.1), custom_call_target="tpu_custom_call" | custom-call | flops 12884901888 | bytes 2097152 | tf_op jit(solution)/shard_map/pallas_call | solution.py:633
  77.4 1.7 %shard_map.60 = (f32[32,2048]{1,0:T(8,128)}, f32[64,256]{1,0:T(8,128)}) custom-call(f32[32,2048]{1,0:T(8,128)} %get-tuple-element.4.a, f32[64,256]{1,0:T(8,128)} %get-tuple-element.5.b), custom_call_target="tpu_custom_call" | custom-call | tf_op jit(solution)/shard_map/pallas_call | solution.py:650
